TPU v7x, 128 devices: a whole 4x4x4 slice. The times are simulated.
128 devices in a mesh: dp: 16 (over z_lo, x, core), tensor: 8 (over y, z_hi).
Axes of the slice: x: 4, y: 4, z: 4 (z_hi: 2, z_lo: 2; z = z_hi * 2 + z_lo), core: 2. Of those that a mesh axis runs over, the one named last changes fastest.
Arguments:
- block_input: bfloat16 [16, 1024, 1024], P('dp', 'tensor'), may hold values from -6 to 6
- segments: int32 [16, 1024], P('dp'), may hold values from 0 to 4, as said below
- first_gain: float32 [1024], replicated, may hold values from 0.5 to 1.5
- mamba_gate: bfloat16 [1024, 1536], P('dp', 'tensor'), may hold values from -0.1875 to 0.1875
- mamba_input: bfloat16 [1024, 1536], P('dp', 'tensor'), may hold values from -0.1875 to 0.1875
- step_weight: bfloat16 [1024, 24], P('dp', 'tensor'), may hold values from -0.1875 to 0.1875
- state_weight: bfloat16 [1024, 256], P(('dp', 'tensor')), may hold values from -0.1875 to 0.1875
- conv_inner: float32 [4, 1536], P(None, 'tensor'), may hold values from -2.5 to 2.5
- conv_state: float32 [4, 256], replicated, may hold values from -2.5 to 2.5
- decay_log: float32 [24], P('tensor'), may hold values from -5.3 to 1.1
- step_bias: float32 [24], P('tensor'), may hold values from -5 to -3
- skip_scale: float32 [24], P('tensor'), may hold values from 0.5 to 1.5
- query_weight: bfloat16 [1024, 512], P('dp', 'tensor'), may hold values from -0.1875 to 0.1875
- keyval_weight: bfloat16 [1024, 256], P(('dp', 'tensor')), may hold values from -0.1875 to 0.1875
- mamba_out: bfloat16 [1536, 1024], P('tensor', 'dp'), may hold values from -0.15625 to 0.15625
- attention_out: bfloat16 [512, 1024], P('tensor', 'dp'), may hold values from -2 to 2
- second_gain: float32 [1024], replicated, may hold values from 0.5 to 1.5
- feed_gate: bfloat16 [1024, 2048], P('dp', 'tensor'), may hold values from -0.1875 to 0.1875
- feed_up: bfloat16 [1024, 2048], P('dp', 'tensor'), may hold values from -0.1875 to 0.1875
- feed_down: bfloat16 [2048, 1024], P('tensor', 'dp'), may hold values from -0.125 to 0.125
- cotangent: bfloat16 [16, 1024, 1024], P('dp', 'tensor'), may hold values from -6 to 6
Outputs:
- block_output: bfloat16 [16, 1024, 1024], P('dp', 'tensor')
- input_grad: float32 [16, 1024, 1024], P('dp', 'tensor')
- first_gain_grad: float32 [1024], replicated
- mamba_gate_grad: float32 [1024, 1536], P('dp', 'tensor')
- mamba_input_grad: float32 [1024, 1536], P('dp', 'tensor')
- step_weight_grad: float32 [1024, 24], P('dp', 'tensor')
- state_weight_grad: float32 [1024, 256], P(('dp', 'tensor'))
- conv_inner_grad: float32 [4, 1536], P(None, 'tensor')
- conv_state_grad: float32 [4, 256], replicated
- decay_log_grad: float32 [24], P('tensor')
- step_bias_grad: float32 [24], P('tensor')
- skip_scale_grad: float32 [24], P('tensor')
- query_weight_grad: float32 [1024, 512], P('dp', 'tensor')
- keyval_weight_grad: float32 [1024, 256], P(('dp', 'tensor'))
- mamba_out_grad: float32 [1536, 1024], P('tensor', 'dp')
- attention_out_grad: float32 [512, 1024], P('tensor', 'dp')
- second_gain_grad: float32 [1024], replicated
- feed_gate_grad: float32 [1024, 2048], P('dp', 'tensor')
- feed_up_grad: float32 [1024, 2048], P('dp', 'tensor')
- feed_down_grad: float32 [2048, 1024], P('tensor', 'dp')
Inputs may be any that keep to these rules, and one draw needn't show every extreme that they name: `segments`: in each row of 1024 positions the numbers start at 0, never fall and rise by one at four places, and segment 2 holds every position from 64 to 959.
All inputs are finite; a program needn't handle non-finite values.
Results may differ from a plain program's by a relative error of at most 0.028.
Values may be sent and summed in bfloat16 or wider, within the bound.
No kernel may reach another device: no remote copies, remote signals or barrier semaphores. Data moves between devices by JAX's collectives and lax.ppermute only.
A program may use at most 192 MiB of HBM per device.

v0:
```python
import jax
import jax.numpy as jnp
from jax import lax
from jax.sharding import PartitionSpec as P

QHEADS = 8
KVHEADS = 2
AHDIM = 64
SSD_BLOCK = 128
QUERY_BLOCK = 512


PRECISE = lax.Precision.HIGHEST
NORM_EPS = 1e-05
ROPE_BASE = 10000.0
MASKED_SCORE = -1e30


def sent_together(arrays, axis, dim, along):
    ends, at = ([], 0)
    for a in arrays[:-1]:
        at += a.shape[along]
        ends.append(at)
    both = jnp.concatenate(arrays, axis=along)
    return tuple(jnp.split(lax.all_gather(both, axis, axis=dim, tiled=True), ends, axis=along))


def rows_first(arrays, axis, dims):
    turned = [jnp.moveaxis(a, dim, 0) for a, dim in zip(arrays, dims)]
    both = jnp.concatenate([t.reshape(len(t), -1) for t in turned], axis=1)
    filled, at, done = (lax.all_gather(both, axis, axis=0, tiled=True), 0, [])
    for t, dim in zip(turned, dims):
        piece = filled[:, at : at + t[0].size].reshape(-1, *t.shape[1:])
        done.append(jnp.moveaxis(piece, 0, dim))
        at += t[0].size
    return tuple(done)


def in_order(blocks, dim):
    dims = list(blocks.shape[1:])
    dims[dim] *= blocks.shape[0]
    return jnp.moveaxis(blocks, 0, dim).reshape(dims)


def copy_for_each(shard, axis):
    copies = jnp.broadcast_to(shard, (lax.axis_size(axis), *shard.shape))
    return lax.all_to_all(copies, axis, split_axis=0, concat_axis=0, tiled=True)


def collect(shard, axis, dim):
    return in_order(copy_for_each(shard, axis), dim)


def cut_along(shard, dim, size):
    before, after = (shard.shape[:dim], shard.shape[dim + 1 :])
    return jnp.moveaxis(shard.reshape(*before, size, -1, *after), dim, 0)


def sum_together(arrays, axis, dims):
    size = lax.axis_size(axis)
    blocks = [cut_along(a, dim, size) for a, dim in zip(arrays, dims)]
    lines = jnp.concatenate([b.reshape(size, -1) for b in blocks], axis=1)
    rows = max(16, -(-lines.shape[1] // 1024) * 8)
    lines = jnp.pad(lines, ((0, 0), (0, rows * 128 - lines.shape[1]))).reshape(-1, 128)
    line, at, done = (lax.psum_scatter(lines, axis, tiled=True).reshape(-1), 0, [])
    for b in blocks:
        part = b[0]
        done.append(line[at : at + part.size].reshape(part.shape))
        at += part.size
    return tuple(done)


def rms_norm(values, scale_vec):
    return (
        values * lax.rsqrt(jnp.mean(values * values, axis=-1, keepdims=True) + NORM_EPS) * scale_vec
    )


def lag_masks(seg_ids, tap_count):
    length = seg_ids.shape[-1]
    mask_list = [jnp.ones(seg_ids.shape, jnp.float32)]
    for lag_step in range(1, tap_count):
        earlier = jnp.concatenate(
            [
                jnp.full(seg_ids.shape[:-1] + (lag_step,), -1, jnp.int32),
                seg_ids[..., : length - lag_step],
            ],
            axis=-1,
        )
        mask_list.append((earlier == seg_ids).astype(jnp.float32))
    return jnp.stack(mask_list)


def conv_silu(values, taps_weight, lag_mask):
    length = values.shape[-2]
    summed = values * taps_weight[0]
    for lag_step in range(1, taps_weight.shape[0]):
        shifted = jnp.concatenate(
            [jnp.zeros_like(values[..., :lag_step, :]), values[..., : length - lag_step, :]],
            axis=-2,
        )
        summed = summed + shifted * lag_mask[lag_step][..., None] * taps_weight[lag_step]
    return jax.nn.silu(summed)


def ssd_block(carried, blocks):
    states, last_seg = carried
    conv_x, input_map, output_map, step_size, decay_step, seg_ids = blocks
    decay_sum = jnp.cumsum(decay_step, axis=1)
    decay_heads = jnp.moveaxis(decay_sum, 2, 1)
    step_heads = jnp.moveaxis(step_size, 2, 1)
    places = jnp.arange(seg_ids.shape[1])
    same_seg = (seg_ids[:, :, None] == seg_ids[:, None, :]) & (places[:, None] >= places[None, :])
    keep_mask = same_seg[:, None]
    decay_gap = decay_heads[:, :, :, None] - decay_heads[:, :, None, :]
    decay_mask = jnp.where(keep_mask, jnp.exp(jnp.where(keep_mask, decay_gap, 0.0)), 0.0)
    intersections = jnp.einsum("rthn,rshn->rhts", output_map, input_map, precision=PRECISE)
    mixing = decay_mask * intersections * step_heads[:, :, None, :]
    inside = jnp.einsum("rhts,rshp->rthp", mixing, conv_x, precision=PRECISE)
    reach_in = (seg_ids == last_seg[:, None]).astype(jnp.float32)[..., None] * jnp.exp(decay_sum)
    incoming = (
        jnp.einsum("rthn,rhpn->rthp", output_map, states, precision=PRECISE) * reach_in[..., None]
    )
    end_seg = seg_ids[:, -1]
    to_end = (
        jnp.exp(decay_sum[:, -1:, :] - decay_sum)
        * (seg_ids == end_seg[:, None]).astype(jnp.float32)[..., None]
        * step_size
    )
    through = jnp.exp(decay_sum[:, -1, :]) * (end_seg == last_seg).astype(jnp.float32)[:, None]
    updated = states * through[:, :, None, None] + jnp.einsum(
        "rsh,rshp,rshn->rhpn", to_end, conv_x, input_map, precision=PRECISE
    )
    return ((updated, end_seg), inside + incoming)


def mamba_core(conv_x, state_maps, gate_raw, step_raw, decay_log, step_bias, skip_scale, seg_ids):
    row_count, length, head_count, map_width = state_maps.shape
    state_size = map_width // 2
    head_dim = conv_x.shape[-1] // head_count
    block_count = length // SSD_BLOCK
    step_size = jax.nn.softplus(step_raw + step_bias)
    decay_step = -step_size * jnp.exp(decay_log)

    def split_blocks(values):
        return jnp.moveaxis(
            values.reshape((row_count, block_count, SSD_BLOCK) + values.shape[2:]), 1, 0
        )

    blocks = (
        split_blocks(conv_x.reshape(row_count, length, head_count, head_dim)),
        split_blocks(state_maps[..., :state_size]),
        split_blocks(state_maps[..., state_size:]),
        split_blocks(step_size),
        split_blocks(decay_step),
        split_blocks(seg_ids),
    )
    initial = (
        jnp.zeros((row_count, head_count, head_dim, state_size), jnp.float32),
        jnp.full((row_count,), -1, jnp.int32),
    )
    final_state, outputs = lax.scan(jax.checkpoint(ssd_block), initial, blocks)
    result = jnp.moveaxis(outputs, 0, 1).reshape(row_count, length, head_count * head_dim)
    result = result + conv_x * jnp.repeat(skip_scale, head_dim)
    return result * jax.nn.silu(gate_raw)


def rope_tables(length, head_dim):
    half_dim = head_dim // 2
    freq_vec = ROPE_BASE ** (-2.0 * jnp.arange(half_dim, dtype=jnp.float32) / head_dim)
    angles = jnp.arange(length, dtype=jnp.float32)[:, None] * freq_vec[None, :]
    angles = jnp.concatenate([angles, angles], axis=-1)
    return (jnp.cos(angles), jnp.sin(angles))


def rotate(values, cosine, sine_tab):
    half_dim = values.shape[-1] // 2
    turned = jnp.concatenate([-values[..., half_dim:], values[..., :half_dim]], axis=-1)
    return values * cosine + turned * sine_tab


def rotate_back(grad_vals, cosine, sine_tab):
    half_dim = grad_vals.shape[-1] // 2
    scaled = grad_vals * sine_tab
    return grad_vals * cosine + jnp.concatenate(
        [scaled[..., half_dim:], -scaled[..., :half_dim]], axis=-1
    )


def flat_dot(left_arr, right_arr):
    return jnp.dot(left_arr, right_arr, preferred_element_type=jnp.float32)


def dot_right(left_arr, right_arr):
    return lax.dot_general(
        left_arr, right_arr, (((1,), (1,)), ((), ())), preferred_element_type=jnp.float32
    )


def dot_left(left_arr, right_arr):
    return lax.dot_general(
        left_arr, right_arr, (((0,), (0,)), ((), ())), preferred_element_type=jnp.float32
    )


def block_scores(query_blk, key_row, seg_row, row_start):
    block_rows = query_blk.shape[0]
    scores = jnp.einsum(
        "bhe,le->hbl", query_blk, key_row, preferred_element_type=jnp.float32
    ) * query_blk.shape[-1] ** (-0.5)
    query_pos = row_start + jnp.arange(block_rows)
    key_pos = jnp.arange(key_row.shape[0])
    query_seg = seg_row[row_start : row_start + block_rows]
    allowed = (query_seg[:, None] == seg_row[None, :]) & (key_pos[None, :] <= query_pos[:, None])
    return jnp.where(allowed[None], scores, MASKED_SCORE)


def attend_row(row_inputs):
    query_row, key_row, value_row, seg_row = row_inputs
    pieces = []
    sums_list = []
    for row_start in range(0, query_row.shape[0], QUERY_BLOCK):
        scores = block_scores(
            query_row[row_start : row_start + QUERY_BLOCK], key_row, seg_row, row_start
        )
        row_top = jnp.max(scores, axis=-1, keepdims=True)
        raised = jnp.exp(scores - row_top)
        row_total = jnp.sum(raised, axis=-1, keepdims=True)
        weights = (raised / row_total).astype(jnp.bfloat16)
        pieces.append(
            jnp.einsum("hbl,le->bhe", weights, value_row, preferred_element_type=jnp.float32)
        )
        sums_list.append((row_top + jnp.log(row_total))[..., 0])
    return (jnp.concatenate(pieces, axis=0), jnp.concatenate(sums_list, axis=1))


def attend_back(row_inputs):
    query_row, key_row, value_row, seg_row, lse_row, grad_row = row_inputs
    head_count = query_row.shape[1]
    scale_val = query_row.shape[-1] ** (-0.5)
    query_grads = []
    key_grad = jnp.zeros((head_count,) + key_row.shape, jnp.float32)
    value_grad = jnp.zeros((head_count,) + value_row.shape, jnp.float32)
    for row_start in range(0, query_row.shape[0], QUERY_BLOCK):
        query_blk = query_row[row_start : row_start + QUERY_BLOCK]
        grad_blk = grad_row[row_start : row_start + QUERY_BLOCK]
        scores = block_scores(query_blk, key_row, seg_row, row_start)
        weights = jnp.exp(scores - lse_row[:, row_start : row_start + QUERY_BLOCK, None])
        weight_grad = jnp.einsum(
            "bhe,le->hbl", grad_blk, value_row, preferred_element_type=jnp.float32
        )
        score_grad = (
            weights * (weight_grad - jnp.sum(weights * weight_grad, axis=-1, keepdims=True))
        ).astype(jnp.bfloat16)
        query_grads.append(
            jnp.einsum("hbl,le->bhe", score_grad, key_row, preferred_element_type=jnp.float32)
            * scale_val
        )
        key_grad = (
            key_grad
            + jnp.einsum("hbl,bhe->hle", score_grad, query_blk, preferred_element_type=jnp.float32)
            * scale_val
        )
        value_grad = value_grad + jnp.einsum(
            "hbl,bhe->hle",
            weights.astype(jnp.bfloat16),
            grad_blk,
            preferred_element_type=jnp.float32,
        )
    return (jnp.concatenate(query_grads, axis=0), key_grad, value_grad)


def body(
    block_input,
    segments,
    first_gain,
    mamba_gate,
    mamba_input,
    step_weight,
    state_weight,
    conv_inner,
    conv_state,
    decay_log,
    step_bias,
    skip_scale,
    query_weight,
    keyval_weight,
    mamba_out,
    attention_out,
    second_gain,
    feed_gate,
    feed_up,
    feed_down,
    cotangent,
):
    tensor_count = lax.axis_size("tensor")
    tensor_index = lax.axis_index("tensor")
    state_full, keyval_full = sent_together((state_weight, keyval_weight), ("dp", "tensor"), 0, 1)
    (
        gate_full,
        input_full,
        step_full,
        query_full,
        mamba_full,
        attend_full,
        feed_gate_full,
        feed_up_full,
        feed_down_full,
    ) = rows_first(
        (
            mamba_gate,
            mamba_input,
            step_weight,
            query_weight,
            mamba_out,
            attention_out,
            feed_gate,
            feed_up,
            feed_down,
        ),
        "dp",
        (0, 0, 0, 0, 1, 1, 0, 0, 1),
    )
    x_piece = block_input.astype(jnp.float32)
    normed_val, first_pullback = jax.vjp(rms_norm, x_piece, first_gain)
    normed = collect(normed_val.astype(jnp.bfloat16), "tensor", 1)
    row_count, length, model_width = normed.shape
    token_count = row_count * length
    normed_flat = normed.reshape(token_count, model_width)
    head_count = decay_log.shape[0]
    inner_width = gate_full.shape[1]
    map_width = state_full.shape[1]
    query_heads = query_full.shape[1] // AHDIM
    kv_head = tensor_index * query_heads // (QHEADS // KVHEADS)
    keyval_here = jnp.concatenate(
        [
            lax.dynamic_slice_in_dim(keyval_full, kv_head * AHDIM, AHDIM, 1),
            lax.dynamic_slice_in_dim(keyval_full, (KVHEADS + kv_head) * AHDIM, AHDIM, 1),
        ],
        axis=1,
    )
    main_weight = jnp.concatenate([gate_full, input_full, step_full, query_full], axis=1)
    projected = flat_dot(
        normed_flat, jnp.concatenate([main_weight, state_full, keyval_here], axis=1)
    ).reshape(row_count, length, -1)
    cut_two = 2 * inner_width
    cut_three = cut_two + head_count
    cut_four = cut_three + query_heads * AHDIM
    cut_five = cut_four + map_width
    gate_raw = projected[..., :inner_width]
    mamba_x = projected[..., inner_width:cut_two]
    step_raw = projected[..., cut_two:cut_three]
    query_raw = projected[..., cut_three:cut_four].reshape(row_count, length, query_heads, AHDIM)
    state_proj = projected[..., cut_four:cut_five]
    keyval_raw = projected[..., cut_five:]
    lag_mask = lag_masks(segments, conv_inner.shape[0])
    copies = jnp.broadcast_to(
        state_proj[:, :, None, :], (row_count, length, head_count, map_width)
    ).reshape(row_count, length, head_count * map_width)

    def conv_piece(conv_values, inner_taps, state_taps):
        return conv_silu(
            conv_values,
            jnp.concatenate([inner_taps, jnp.tile(state_taps, (1, head_count))], axis=-1),
            lag_mask,
        )

    conv_out, conv_pullback = jax.vjp(
        conv_piece, jnp.concatenate([mamba_x, copies], axis=-1), conv_inner, conv_state
    )
    conv_low = lax.optimization_barrier(conv_out.astype(jnp.bfloat16)).astype(jnp.float32)

    def core_piece(conv_vals, map_vals, gate_vals, step_vals, decay_vals, bias_vals, skip_vals):
        return mamba_core(
            conv_vals, map_vals, gate_vals, step_vals, decay_vals, bias_vals, skip_vals, segments
        )

    gated_out, core_pullback = jax.vjp(
        core_piece,
        conv_low[..., :inner_width],
        conv_low[..., inner_width:].reshape(row_count, length, head_count, map_width),
        gate_raw,
        step_raw,
        decay_log,
        step_bias,
        skip_scale,
    )
    gated_low = gated_out.astype(jnp.bfloat16).reshape(token_count, inner_width)
    cosine, sine_tab = rope_tables(length, AHDIM)
    queries = rotate(query_raw, cosine[:, None], sine_tab[:, None]).astype(jnp.bfloat16)
    keys_low = rotate(keyval_raw[..., :AHDIM], cosine, sine_tab).astype(jnp.bfloat16)
    values_low = keyval_raw[..., AHDIM:].astype(jnp.bfloat16)
    attended, log_sums = lax.map(attend_row, (queries, keys_low, values_low, segments))
    attended_low = attended.astype(jnp.bfloat16).reshape(token_count, query_heads * AHDIM)
    mix_terms = flat_dot(gated_low, mamba_full) + flat_dot(attended_low, attend_full)
    hidden = x_piece + lax.psum_scatter(
        mix_terms.reshape(row_count, length, model_width).astype(jnp.bfloat16),
        "tensor",
        scatter_dimension=1,
        tiled=True,
    ).astype(jnp.float32)
    normed_two_val, second_pullback = jax.vjp(rms_norm, hidden, second_gain)
    normed_two = collect(normed_two_val.astype(jnp.bfloat16), "tensor", 1)
    normed_two_flat = normed_two.reshape(token_count, model_width)
    gate_proj = flat_dot(normed_two_flat, feed_gate_full)
    up_proj = flat_dot(normed_two_flat, feed_up_full)
    sigmoid_gate = jax.nn.sigmoid(gate_proj)
    silu_gate = gate_proj * sigmoid_gate
    activation = (silu_gate * up_proj).astype(jnp.bfloat16)
    block_out = hidden + lax.psum_scatter(
        flat_dot(activation, feed_down_full)
        .reshape(row_count, length, model_width)
        .astype(jnp.bfloat16),
        "tensor",
        scatter_dimension=1,
        tiled=True,
    ).astype(jnp.float32)
    out_grad = cotangent.astype(jnp.float32)
    out_grad_all = collect(cotangent, "tensor", 1).reshape(token_count, model_width)
    act_grad = dot_right(out_grad_all, feed_down_full)
    feed_down_grad = dot_left(activation, out_grad_all)
    up_grad = (act_grad * silu_gate).astype(jnp.bfloat16)
    gate_grad = (act_grad * up_proj * (sigmoid_gate + silu_gate * (1.0 - sigmoid_gate))).astype(
        jnp.bfloat16
    )
    feed_gate_grad = dot_left(normed_two_flat, gate_grad)
    feed_up_grad = dot_left(normed_two_flat, up_grad)
    normed_two_grad = dot_right(gate_grad, feed_gate_full) + dot_right(up_grad, feed_up_full)
    normed_two_piece = lax.psum_scatter(
        normed_two_grad.reshape(row_count, length, model_width).astype(jnp.bfloat16),
        "tensor",
        scatter_dimension=1,
        tiled=True,
    ).astype(jnp.float32)
    hidden_norm_grad, second_gain_grad = second_pullback(normed_two_piece)
    hidden_grad = out_grad + hidden_norm_grad
    mix_grad = collect(hidden_grad.astype(jnp.bfloat16), "tensor", 1).reshape(
        token_count, model_width
    )
    gated_grad = dot_right(mix_grad, mamba_full).reshape(row_count, length, inner_width)
    mamba_out_grad = dot_left(gated_low, mix_grad)
    attend_grad = (
        dot_right(mix_grad, attend_full)
        .astype(jnp.bfloat16)
        .reshape(row_count, length, query_heads, AHDIM)
    )
    attend_out_grad = dot_left(attended_low, mix_grad)
    conv_x_grad, maps_grad, gate_raw_grad, step_raw_grad, decay_grad, bias_grad, skip_grad = (
        core_pullback(gated_grad)
    )
    conv_in_grad, inner_taps_grad, state_taps_grad = conv_pullback(
        jnp.concatenate([conv_x_grad, maps_grad.reshape(row_count, length, -1)], axis=-1)
    )
    query_rot_grad, key_rot_grad, value_grad = lax.map(
        attend_back, (queries, keys_low, values_low, segments, log_sums, attend_grad)
    )
    query_grad = rotate_back(query_rot_grad, cosine[:, None], sine_tab[:, None])
    key_grad = rotate_back(key_rot_grad, cosine, sine_tab)
    main_grad = (
        jnp.concatenate(
            [
                gate_raw_grad,
                conv_in_grad[..., :inner_width],
                step_raw_grad,
                query_grad.reshape(row_count, length, -1),
            ],
            axis=-1,
        )
        .astype(jnp.bfloat16)
        .reshape(token_count, -1)
    )
    copy_grad = (
        conv_in_grad[..., inner_width:]
        .reshape(row_count, length, head_count, map_width)
        .astype(jnp.bfloat16)
    )
    keyval_grad = jnp.concatenate([key_grad, value_grad], axis=-1).astype(jnp.bfloat16)
    normed_grad = dot_right(main_grad, main_weight)
    normed_grad = normed_grad + jnp.einsum(
        "rlhc,dc->rld", copy_grad, state_full, preferred_element_type=jnp.float32
    ).reshape(token_count, model_width)
    normed_grad = normed_grad + jnp.einsum(
        "rhlf,df->rld", keyval_grad, keyval_here, preferred_element_type=jnp.float32
    ).reshape(token_count, model_width)
    main_weight_grad = dot_left(normed_flat, main_grad)
    state_grad = jnp.einsum("rld,rlhc->dc", normed, copy_grad, preferred_element_type=jnp.float32)
    keyval_here_grad = jnp.einsum(
        "rld,rhlf->df", normed, keyval_grad, preferred_element_type=jnp.float32
    )
    keyval_grad_full = jnp.zeros(keyval_full.shape, jnp.float32)
    keyval_grad_full = lax.dynamic_update_slice_in_dim(
        keyval_grad_full, keyval_here_grad[:, :AHDIM], kv_head * AHDIM, 1
    )
    keyval_grad_full = lax.dynamic_update_slice_in_dim(
        keyval_grad_full, keyval_here_grad[:, AHDIM:], (KVHEADS + kv_head) * AHDIM, 1
    )
    normed_piece = lax.psum_scatter(
        normed_grad.reshape(row_count, length, model_width).astype(jnp.bfloat16),
        "tensor",
        scatter_dimension=1,
        tiled=True,
    ).astype(jnp.float32)
    input_norm_grad, first_gain_grad = first_pullback(normed_piece)
    input_grad = hidden_grad + input_norm_grad
    conv_whole = lax.dynamic_update_slice_in_dim(
        jnp.zeros((inner_taps_grad.shape[0], inner_width * tensor_count), jnp.float32),
        inner_taps_grad,
        tensor_index * inner_width,
        1,
    )
    head_whole = lax.dynamic_update_slice_in_dim(
        jnp.zeros((3, head_count * tensor_count), jnp.float32),
        jnp.stack([decay_grad, bias_grad, skip_grad]),
        tensor_index * head_count,
        1,
    )
    state_sum, keyval_sum, first_gain_sum, second_gain_sum, conv_sum, conv_state_sum, head_sum = (
        lax.psum(
            (
                state_grad,
                keyval_grad_full,
                first_gain_grad,
                second_gain_grad,
                conv_whole,
                state_taps_grad,
                head_whole,
            ),
            ("dp", "tensor"),
        )
    )
    flat_index = lax.axis_index(("dp", "tensor"))
    share_rows = state_weight.shape[0]
    state_out_grad = lax.dynamic_slice_in_dim(state_sum, flat_index * share_rows, share_rows, 0)
    keyval_out_grad = lax.dynamic_slice_in_dim(keyval_sum, flat_index * share_rows, share_rows, 0)
    conv_out_grad = lax.dynamic_slice_in_dim(conv_sum, tensor_index * inner_width, inner_width, 1)
    head_part = lax.dynamic_slice_in_dim(head_sum, tensor_index * head_count, head_count, 1)
    gate_weight_grad = main_weight_grad[:, :inner_width]
    input_weight_grad = main_weight_grad[:, inner_width:cut_two]
    step_weight_grad = main_weight_grad[:, cut_two:cut_three]
    query_weight_grad = main_weight_grad[:, cut_three:cut_four]
    (
        gate_sum,
        input_sum,
        step_sum,
        query_sum,
        mamba_sum,
        attend_sum,
        feed_gate_sum,
        feed_up_sum,
        feed_down_sum,
    ) = tuple(
        (
            part.astype(jnp.float32)
            for part in sum_together(
                (
                    gate_weight_grad.astype(jnp.bfloat16),
                    input_weight_grad.astype(jnp.bfloat16),
                    step_weight_grad.astype(jnp.bfloat16),
                    query_weight_grad.astype(jnp.bfloat16),
                    mamba_out_grad.astype(jnp.bfloat16),
                    attend_out_grad.astype(jnp.bfloat16),
                    feed_gate_grad.astype(jnp.bfloat16),
                    feed_up_grad.astype(jnp.bfloat16),
                    feed_down_grad.astype(jnp.bfloat16),
                ),
                "dp",
                (0, 0, 0, 0, 1, 1, 0, 0, 1),
            )
        )
    )
    return (
        block_out.astype(jnp.bfloat16),
        input_grad,
        first_gain_sum,
        gate_sum,
        input_sum,
        step_sum,
        state_out_grad,
        conv_out_grad,
        conv_state_sum,
        head_part[0],
        head_part[1],
        head_part[2],
        query_sum,
        keyval_out_grad,
        mamba_sum,
        attend_sum,
        second_gain_sum,
        feed_gate_sum,
        feed_up_sum,
        feed_down_sum,
    )


def solution(mesh):
    in_specs = (
        P("dp", "tensor", None),
        P("dp", None),
        P(),
        P("dp", "tensor"),
        P("dp", "tensor"),
        P("dp", "tensor"),
        P(("dp", "tensor"), None),
        P(None, "tensor"),
        P(),
        P("tensor"),
        P("tensor"),
        P("tensor"),
        P("dp", "tensor"),
        P(("dp", "tensor"), None),
        P("tensor", "dp"),
        P("tensor", "dp"),
        P(),
        P("dp", "tensor"),
        P("dp", "tensor"),
        P("tensor", "dp"),
        P("dp", "tensor", None),
    )
    out_specs = (
        P("dp", "tensor", None),
        P("dp", "tensor", None),
        P(),
        P("dp", "tensor"),
        P("dp", "tensor"),
        P("dp", "tensor"),
        P(("dp", "tensor"), None),
        P(None, "tensor"),
        P(),
        P("tensor"),
        P("tensor"),
        P("tensor"),
        P("dp", "tensor"),
        P(("dp", "tensor"), None),
        P("tensor", "dp"),
        P("tensor", "dp"),
        P(),
        P("dp", "tensor"),
        P("dp", "tensor"),
        P("tensor", "dp"),
    )
    return jax.shard_map(body, mesh=mesh, in_specs=in_specs, out_specs=out_specs, check_vma=False)
```

profile of v0, /device:TPU:0, one launch (start us, length us, event | category | flops | bytes accessed | tf_op | source)
XLA Modules:
  0.0 1768.2 jit_solution(2147673889627383992)
XLA Ops:
  16.8 7.9 all-to-all-start
  28.2 279.8 %all-gather.5.cloned.1.call-done = bf16[1024,512]{1,0:T(8,128)(2,1)} async-done(((bf16[8,512]{1,0:T(8,128)(2,1)}), bf16[1024,512]{1,0:T(8,128)(2,1)}) %all-gather.5.cloned.1.call-update) | async-done | bytes 1048592 | tf_op jit(solution)/shard_map/all_gather | solution.py:25
  310.3 37.6 %all-gather.3.cloned.1.call-done = bf16[1024,1475]{1,0:T(8,128)(2,1)} async-done(((bf16[64,1475]{1,0:T(8,128)(2,1)}), bf16[1024,1475]{1,0:T(8,128)(2,1)}) %all-gather.3.cloned.1.call-update) | async-done | bytes 3020816 | tf_op jit(solution)/shard_map/all_gather | solution.py:31
  350.2 4.5 convolution_bitcast_fusion.9
  359.2 5.7 multiply_convert_fusion
  400.4 157.9 %while.57 = (s32[]{:T(128)}, f32[1,3,64,128]{3,2,1,0:T(8,128)S(1)}, s32[1]{0:T(128)}, f32[8,1,128,3,64]{2,0,4,3,1:T(8,128)}, f32[8,1,3,64,128]{4,3,2,1,0:T(8,128...) while((s32[]{:T(128)}, f32[1,3,64,128]{3,2,1,0:T(8,128)S(1)}, ...), condition=%wide.region_3.4_spmd.clone, body=%wide.region_1.3_spmd.clone.sunk | while | flops 189286016 | bytes 2436934 | solution.py:162
  413.6 3.8 dynamic_update_slice.117
  433.4 3.8 dynamic_update_slice.117
  453.1 3.8 dynamic_update_slice.117
  472.9 3.8 dynamic_update_slice.117
  492.7 3.8 dynamic_update_slice.117
  512.4 3.8 dynamic_update_slice.117
  532.2 3.8 dynamic_update_slice.117
  551.9 3.8 dynamic_update_slice.117
  567.8 75.9 %reduce-scatter.5.cloned.1.call-done = bf16[1,128,1024]{2,1,0:T(8,128)(2,1)} async-done(((bf16[1,1024,1024]{2,1,0:T(8,128)(2,1)}), bf16[1,128,1024]{2,1,0:T(8,128)(2,1)}) %reduce-scatter.5.cloned.1.call-update) | async-done | bytes 262160 | tf_op jit(solution)/shard_map/reduce_scatter | solution.py:396
  646.1 31.0 %all_to_all.20 = bf16[8,1,128,1024]{3,2,1,0:T(8,128)(2,1)} all-to-all(bf16[8,1,128,1024]{3,2,1,0:T(8,128)(2,1)S(1)} %broadcast_in_dim.305), channel_id=1, replica_groups=mesh['dp'=16,'tensor'=8] {'tensor'}, dimensions={0} | all-to-all | bytes 4194304 | tf_op jit(solution)/shard_map/all_to_all | solution.py:47
  678.7 4.3 all-to-all-start.2
  683.1 3.7 fusion.174
  689.8 19.9 %all-to-all-done.2 = bf16[8,1,128,1024]{3,2,1,0:T(8,128)(2,1)} async-done(((bf16[8,1,128,1024]{3,2,1,0:T(8,128)(2,1)}), bf16[8,1,128,1024]{3,2,1,0:T(8,128)(2,1)}, u32[]{:S(2)}, u32[]{:S(2)}) %all-to-all-start.2) | async-done | bytes 2097184 | tf_op jit(solution)/shard_map/all_to_all | solution.py:47
  709.7 4.3 multiply_convert_fusion.1
  720.1 72.0 %reduce-scatter.9.cloned.1.call-done = bf16[1,128,1024]{2,1,0:T(8,128)(2,1)} async-done(((bf16[1,1024,1024]{2,1,0:T(8,128)(2,1)}), bf16[1,128,1024]{2,1,0:T(8,128)(2,1)}) %reduce-scatter.9.cloned.1.call-update) | async-done | bytes 262160 | tf_op jit(solution)/shard_map/reduce_scatter | solution.py:429
  796.9 4.4 all-to-all-start.3
  803.9 3.4 convolution_convert_fusion.1
  814.6 3.3 convolution_convert_fusion.3
  825.3 4.9 all-to-all-done.3
  851.8 405.2 %while.58 = (s32[]{:T(128)}, f32[1,3,64,128]{3,2,1,0:T(8,128)}, f32[8,1,128,3,64]{2,0,4,3,1:T(8,128)}, f32[8,1,128,3,128]{4,2,0,3,1:T(8,128)}, f32[8,1,128,3,128...) while((s32[]{:T(128)}, f32[1,3,64,128]{3,2,1,0:T(8,128)}, ...), condition=%wide.region_22.23_spmd.clone, body=%wide.region_13.22_spmd.clone.sunk | while | flops 492705536 | bytes 9536757 | solution.py:162
  895.0 3.8 dynamic_update_slice.121
  945.7 3.8 dynamic_update_slice.121
  996.5 3.8 dynamic_update_slice.121
  1047.2 3.8 dynamic_update_slice.121
  1097.9 3.8 dynamic_update_slice.121
  1148.7 3.8 dynamic_update_slice.121
  1199.4 3.8 dynamic_update_slice.121
  1250.1 3.8 dynamic_update_slice.121
  1259.0 4.5 multiply_reduce_fusion.6
  1265.5 3.6 copy.383
  1269.1 9.9 multiply_reduce_fusion.5
  1316.9 4.0 dynamic_update_slice.95
  1328.8 3.8 dynamic-update-slice.4
  1334.7 4.9 dynamic-update-slice.6
  1339.6 4.9 dynamic-update-slice.7
  1344.5 4.5 dynamic-update-slice.8
  1365.7 107.7 %all-reduce.25.cloned.1.call-done = (f32[1024,256]{1,0:T(8,128)}, f32[1024,256]{1,0:T(8,128)}) async-done(((f32[1024,256]{1,0:T(8,128)}, f32[1024,256]{1,0:T(8,128)}), (f32[1024,256]{1,0:T(8,128)}, f32[1024,256]{1,0:T(8,128)})) %all-reduce.25.cloned.1.call-update) | async-done | bytes 2097168 | tf_op jit(solution)/shard_map/psum | solution.py:518
  1474.7 124.9 %all-reduce.23.cloned.1.call-done = bf16[11904,128]{1,0:T(8,128)(2,1)} async-done(((bf16[11904,128]{1,0:T(8,128)(2,1)}), bf16[11904,128]{1,0:T(8,128)(2,1)}) %all-reduce.23.cloned.1.call-update) | async-done | bytes 3047440
  1600.9 21.1 %slice.322 = bf16[31744,3]{1,0:T(8,128)(2,1)} reshape(bf16[744,128]{1,0:T(8,128)(2,1)S(1)} %constant_dynamic-slice_fusion.12) | data formatting | bytes 380928 | tf_op jit(solution)/shard_map/slice | solution.py:68
  1630.0 50.5 %reduce-scatter.11.cloned.1.call-done = bf16[1,128,1024]{2,1,0:T(8,128)(2,1)} async-done(((bf16[1,1024,1024]{2,1,0:T(8,128)(2,1)}), bf16[1,128,1024]{2,1,0:T(8,128)(2,1)}) %reduce-scatter.11.cloned.1.call-update) | async-done | bytes 262160 | tf_op jit(solution)/shard_map/reduce_scatter | solution.py:497
  1681.7 66.6 %all-reduce.18 = (f32[1024]{0:T(1024)}, f32[4,1536]{1,0:T(4,128)S(1)}, f32[4,256]{1,0:T(4,128)}, f32[3,24]{1,0:T(4,128)S(1)}, f32[1024]{0:T(1024)}) all-reduce(f32[1024]{0:T(1024)S(1)} %get-tuple-element.999, f32[4,1536]{1,0:T(4,128)S(1)} %dynamic_update_slice.93, ...), channel_id=1, replica_groups=mesh['dp'=16,'tensor'=8] {'dp','tensor'}, use_global_device_ids=true, to_apply=%region_29.30 | all-reduce | flops 9288 | bytes 74304 | tf_op jit(solution)/shard_map/psum | solution.py:518
  1749.6 9.3 reduce-scatter.7.cloned.1.call-done
  (1086 shorter events, 685.2 us)
Async XLA Ops:
  7.2 300.8 %all-gather.5.cloned.1.call-start = ((), (), s32[]{:S(2)}) async-start(), calls=%async_computation.9 | async-start | bytes 1056768 | tf_op jit(solution)/shard_map/all_gather | solution.py:25
  8.6 339.4 %all-gather.3.cloned.1.call-start = ((), (), s32[]{:S(2)}) async-start(), calls=%async_computation.8 | async-start | bytes 3342336 | tf_op jit(solution)/shard_map/all_gather | solution.py:31
  16.8 333.4 %all-to-all-start = ((bf16[8,1,128,1024]{3,2,1,0:T(8,128)(2,1)}), bf16[8,1,128,1024]{3,2,1,0:T(8,128)(2,1)S(1)}, u32[]{:S(2)}, u32[]{:S(2)}) async-start(bf16[8,1,128,1024]{3,2,1,0:T(8,128)(2,1)} %broadcast_in_dim.300), calls=%async_computation | async-start | bytes 4194304 | tf_op jit(solution)/shard_map/all_to_all | solution.py:47
  24.7 619.0 %reduce-scatter.5.cloned.1.call-start = ((), (), s32[]{:S(2)}) async-start(), calls=%async_computation.10 | async-start | bytes 2359296 | tf_op jit(solution)/shard_map/reduce_scatter | solution.py:396
  24.8 344.6 %copy-start.120 = (f32[3]{0:T(128)}, f32[3]{0:T(128)S(1)}, u32[]{:S(2)}) copy-start(f32[3]{0:T(128)S(1)} %exp.179) | copy-start | bytes 40
  25.7 330.8 %copy-start.88 = (f32[1,960]{1,0:T(1,128)}, f32[1,960]{1,0:T(1,128)S(1)}, u32[]{:S(2)}) copy-start(f32[1,960]{1,0:T(1,128)S(1)} %get-tuple-element.1125) | copy-start | bytes 11524
  25.7 330.8 %copy-start.90 = (f32[1,960]{1,0:T(1,128)}, f32[1,960]{1,0:T(1,128)S(1)}, u32[]{:S(2)}) copy-start(f32[1,960]{1,0:T(1,128)S(1)} %get-tuple-element.1127) | copy-start | bytes 11524
  25.7 330.8 %copy-start.92 = (f32[1,960]{1,0:T(1,128)}, f32[1,960]{1,0:T(1,128)S(1)}, u32[]{:S(2)}) copy-start(f32[1,960]{1,0:T(1,128)S(1)} %get-tuple-element.1128) | copy-start | bytes 11524
  25.7 330.8 %copy-start.94 = (f32[1,960]{1,0:T(1,128)}, f32[1,960]{1,0:T(1,128)S(1)}, u32[]{:S(2)}) copy-start(f32[1,960]{1,0:T(1,128)S(1)} %get-tuple-element.1126) | copy-start | bytes 11524
  27.4 773.9 %copy-start.81 = (f32[1,1024]{1,0:T(1,128)}, f32[1,1024]{1,0:T(1,128)S(1)}, u32[]{:S(2)}) copy-start(f32[1,1024]{1,0:T(1,128)S(1)} %get-tuple-element.1132) | copy-start | bytes 12292
  27.4 774.6 %copy-start.79 = (f32[1,1024]{1,0:T(1,128)}, f32[1,1024]{1,0:T(1,128)S(1)}, u32[]{:S(2)}) copy-start(f32[1,1024]{1,0:T(1,128)S(1)} %get-tuple-element.1131) | copy-start | bytes 12292
  27.4 775.2 %copy-start.83 = (f32[1,1024]{1,0:T(1,128)}, f32[1,1024]{1,0:T(1,128)S(1)}, u32[]{:S(2)}) copy-start(f32[1,1024]{1,0:T(1,128)S(1)} %get-tuple-element.1133) | copy-start | bytes 12292
  28.2 346.0 %copy-start.49 = (f32[1,1024,1,32]{1,3,2,0:T(8,128)}, f32[1,1024,1,32]{1,3,2,0:T(8,128)S(1)}, u32[]{:S(2)}) copy-start(f32[1,1024,1,32]{1,3,2,0:T(8,128)S(1)} %get-tuple-element.1138) | copy-start | bytes 393220
  310.3 44.4 %copy-start.55 = (bf16[1024,64]{1,0:T(8,128)(2,1)}, bf16[1024,64]{1,0:T(8,128)(2,1)S(1)}, u32[]{:S(2)}) copy-start(bf16[1024,64]{1,0:T(8,128)(2,1)S(1)} %get-tuple-element.1110) | copy-start | bytes 393220
  310.3 44.4 %copy-start.56 = (bf16[1024,64]{1,0:T(8,128)(2,1)}, bf16[1024,64]{1,0:T(8,128)(2,1)S(1)}, u32[]{:S(2)}) copy-start(bf16[1024,64]{1,0:T(8,128)(2,1)S(1)} %get-tuple-element.1111) | copy-start | bytes 393220
  354.7 16.7 copy-start.17
  379.7 185.0 %copy-start.68 = (bf16[64,512]{1,0:T(8,128)(2,1)}, bf16[64,512]{1,0:T(8,128)(2,1)S(1)}, u32[]{:S(2)}) copy-start(bf16[64,512]{1,0:T(8,128)(2,1)S(1)} %convolution_convert_fusion.7) | copy-start | bytes 196612
  383.2 181.5 %copy-start.70 = (bf16[64,512]{1,0:T(8,128)(2,1)}, bf16[64,512]{1,0:T(8,128)(2,1)S(1)}, u32[]{:S(2)}) copy-start(bf16[64,512]{1,0:T(8,128)(2,1)S(1)} %convolution_convert_fusion.8) | copy-start | bytes 196612
  564.6 79.0 %copy-start.14 = (bf16[1,128,1024]{2,1,0:T(8,128)(2,1)S(1)}, bf16[1,128,1024]{2,1,0:T(8,128)(2,1)}, u32[]{:S(2)}) copy-start(bf16[1,128,1024]{2,1,0:T(8,128)(2,1)} %param.25) | copy-start | bytes 786436
  564.7 80.1 %copy-start.77 = (f32[1024]{0:T(1024)S(1)}, f32[1024]{0:T(1024)}, u32[]{:S(2)}) copy-start(f32[1024]{0:T(1024)} %param.41) | copy-start | bytes 12292
  644.8 149.1 %copy-start.111 = (f32[128]{0:T(128)}, f32[128]{0:T(128)S(1)}, u32[]{:S(2)}) copy-start(f32[128]{0:T(128)S(1)} %fusion.249) | copy-start | bytes 1540
  645.9 31.3 %copy-start.30 = (bf16[1,128,1024]{2,1,0:T(8,128)(2,1)S(1)}, bf16[1,128,1024]{2,1,0:T(8,128)(2,1)}, u32[]{:S(2)}) copy-start(bf16[1,128,1024]{2,1,0:T(8,128)(2,1)} %param.45) | copy-start | bytes 786436
  678.7 31.0 %all-to-all-start.2 = ((bf16[8,1,128,1024]{3,2,1,0:T(8,128)(2,1)}), bf16[8,1,128,1024]{3,2,1,0:T(8,128)(2,1)}, u32[]{:S(2)}, u32[]{:S(2)}) async-start(bf16[8,1,128,1024]{3,2,1,0:T(8,128)(2,1)} %broadcast_in_dim.306), calls=%async_computation.4 | async-start | bytes 4194304 | tf_op jit(solution)/shard_map/all_to_all | solution.py:47
  683.1 108.9 %reduce-scatter.9.cloned.1.call-start = ((), (), s32[]{:S(2)}) async-start(), calls=%async_computation.12 | async-start | bytes 2359296 | tf_op jit(solution)/shard_map/reduce_scatter | solution.py:429
  796.9 33.4 %all-to-all-start.3 = ((bf16[8,1,128,1024]{3,2,1,0:T(8,128)(2,1)}), bf16[8,1,128,1024]{3,2,1,0:T(8,128)(2,1)}, u32[]{:S(2)}, u32[]{:S(2)}) async-start(bf16[8,1,128,1024]{3,2,1,0:T(8,128)(2,1)} %broadcast_in_dim.308), calls=%async_computation.6 | async-start | bytes 4194304 | tf_op jit(solution)/shard_map/all_to_all | solution.py:47
  801.2 672.2 %all-reduce.25.cloned.1.call-start = ((), (), s32[]{:S(2)}) async-start(), calls=%async_computation.15 | async-start | bytes 4194304 | tf_op jit(solution)/shard_map/psum | solution.py:518
  903.7 16.0 copy-start.75
  954.4 16.0 copy-start.75
  1055.9 16.0 copy-start.75
  1157.3 16.0 copy-start.75
  1208.1 16.0 copy-start.75
  1316.9 17.8 %copy-start.35 = (bf16[16,16384]{1,0:T(8,128)(2,1)S(1)}, bf16[16,16384]{1,0:T(8,128)(2,1)}, u32[]{:S(2)}) copy-start(bf16[16,16384]{1,0:T(8,128)(2,1)} %reshape_reshape.22) | copy-start | bytes 1572868
  1320.9 18.7 %copy-start.36 = (bf16[16,16384]{1,0:T(8,128)(2,1)S(1)}, bf16[16,16384]{1,0:T(8,128)(2,1)}, u32[]{:S(2)}) copy-start(bf16[16,16384]{1,0:T(8,128)(2,1)} %reshape_reshape.23) | copy-start | bytes 1572868
  1323.4 21.1 %copy-start.33 = (bf16[16,16384]{1,0:T(8,128)(2,1)S(1)}, bf16[16,16384]{1,0:T(8,128)(2,1)}, u32[]{:S(2)}) copy-start(bf16[16,16384]{1,0:T(8,128)(2,1)} %reshape.2145) | copy-start | bytes 1572868
  1324.5 275.2 %all-reduce.23.cloned.1.call-start = ((), (), s32[]{:S(2)}) async-start(), calls=%async_computation.14 | async-start | bytes 6094848
  1353.8 326.7 %reduce-scatter.11.cloned.1.call-start = ((), (), s32[]{:S(2)}) async-start(), calls=%async_computation.13 | async-start | bytes 2359296 | tf_op jit(solution)/shard_map/reduce_scatter | solution.py:497
  1360.3 398.5 %reduce-scatter.7.cloned.1.call-start = ((), (), s32[]{:S(2)}) async-start(), calls=%async_computation.11 | async-start | bytes 2359296 | tf_op jit(solution)/shard_map/reduce_scatter | solution.py:410
  1600.8 79.8 %copy-start.15 = (bf16[1,128,1024]{2,1,0:T(8,128)(2,1)S(1)}, bf16[1,128,1024]{2,1,0:T(8,128)(2,1)}, u32[]{:S(2)}) copy-start(bf16[1,128,1024]{2,1,0:T(8,128)(2,1)} %param.25) | copy-start | bytes 786436
  1600.8 79.8 %copy-start.87 = (f32[1024]{0:T(1024)S(1)}, f32[1024]{0:T(1024)}, u32[]{:S(2)}) copy-start(f32[1024]{0:T(1024)} %param.27) | copy-start | bytes 12292
  1600.8 79.8 %copy-start.114 = (f32[128]{0:T(128)S(1)}, f32[128]{0:T(128)}, u32[]{:S(2)}) copy-start(f32[128]{0:T(128)} %copy-done.113) | copy-start | bytes 1540
  1600.8 81.0 %copy-start.97 = (f32[1024]{0:T(1024)S(1)}, f32[1024]{0:T(1024)}, u32[]{:S(2)}) copy-start(f32[1024]{0:T(1024)} %get-tuple-element.997) | copy-start | bytes 12292
  1600.8 148.3 %copy-start.126 = (f32[128]{0:T(128)S(1)}, f32[128]{0:T(128)}, u32[]{:S(2)}) copy-start(f32[128]{0:T(128)} %copy-done.125) | copy-start | bytes 1540
  1600.8 158.1 %copy-start.19 = (bf16[1,128,1024]{2,1,0:T(8,128)(2,1)S(1)}, bf16[1,128,1024]{2,1,0:T(8,128)(2,1)}, u32[]{:S(2)}) copy-start(bf16[1,128,1024]{2,1,0:T(8,128)(2,1)} %reduce-scatter.5.cloned.1.call-done) | copy-start | bytes 786436
  1600.8 158.0 %copy-start.31 = (bf16[1,128,1024]{2,1,0:T(8,128)(2,1)S(1)}, bf16[1,128,1024]{2,1,0:T(8,128)(2,1)}, u32[]{:S(2)}) copy-start(bf16[1,128,1024]{2,1,0:T(8,128)(2,1)} %param.45) | copy-start | bytes 786436
  1600.8 158.0 %copy-start.32 = (bf16[1,128,1024]{2,1,0:T(8,128)(2,1)S(1)}, bf16[1,128,1024]{2,1,0:T(8,128)(2,1)}, u32[]{:S(2)}) copy-start(bf16[1,128,1024]{2,1,0:T(8,128)(2,1)} %reduce-scatter.9.cloned.1.call-done) | copy-start | bytes 786436
  1600.8 158.0 %copy-start.78 = (f32[1024]{0:T(1024)S(1)}, f32[1024]{0:T(1024)}, u32[]{:S(2)}) copy-start(f32[1024]{0:T(1024)} %param.41) | copy-start | bytes 12292
  1600.9 158.0 %copy-start.112 = (f32[128]{0:T(128)S(1)}, f32[128]{0:T(128)}, u32[]{:S(2)}) copy-start(f32[128]{0:T(128)} %copy-done.111) | copy-start | bytes 1540
  1600.9 158.0 %copy-start.124 = (f32[128]{0:T(128)S(1)}, f32[128]{0:T(128)}, u32[]{:S(2)}) copy-start(f32[128]{0:T(128)} %copy-done.123) | copy-start | bytes 1540
  (151 other events, 870.9 us)
Sparse Core Ops, SparseCore 0:
  10.3 297.6 all-gather.4
  309.7 38.1 all-gather.2
  567.9 75.6 reduce-scatter.4
  720.2 71.7 reduce-scatter.8
  1324.6 148.7 all-reduce.24
  1475.8 123.7 all-reduce.22
  1603.4 77.0 reduce-scatter.10
  1684.8 74.0 reduce-scatter.6
where the time goes:
time: 1790 us; the launch traced here: 1770 us
  waiting for transfers between devices  783 us (44%)
  local copies, waits for them, and re-layouts  413 us (23%)
  matrix products  239 us (13%)
  other arithmetic  180 us (10%)
  blocking collectives  97.6 us (5%)
  loops' own time  22.3 us (1%)
    all_gather x1, waiting for transfers between devices, sent_together(): lax.all_gather(both, axis, axis=dim, tiled=True)  280 us
    unnamed x9, waiting for transfers between devices  125 us
    dynamic_update_slice x72, local copies, waits for them, and re-layouts, mamba_core(): final_state, outputs = lax.scan(jax.checkpoint(ssd_block), initial, blocks)  112 us
    psum x1, waiting for transfers between devices, body(): lax.psum((state_grad, keyval_grad_full, first_gain_grad, second_gain_grad...  108 us
    squeeze x64, local copies, waits for them, and re-layouts, mamba_core(): final_state, outputs = lax.scan(jax.checkpoint(ssd_block), initial, blocks)  77.4 us
    reduce_scatter x1, waiting for transfers between devices, body(): lax.psum_scatter(mix_terms.reshape(row_count, length, model_width).astype...  75.9 us
    reduce_scatter x1, waiting for transfers between devices, body(): lax.psum_scatter(normed_two_grad.reshape(row_count, length, model_width)....  72 us
    psum x1, blocking collectives, body(): lax.psum((state_grad, keyval_grad_full, first_gain_grad, second_gain_grad...  66.6 us
  transfers between devices with their start and end apart: 11, of which 10 were waited for; matrix products, arithmetic and copies ran while one was open for 7% of the time, Pallas kernels for 0%

commit v1 on v0

v1 whole, which is shorter than its diff:
```python
import jax
import jax.numpy as jnp
from jax import lax
from jax.experimental import pallas as pl
from jax.experimental.pallas import tpu as pltpu
from jax.sharding import PartitionSpec as P

QHEADS = 8
KVHEADS = 2
AHDIM = 64
TOKENS = 1024
WIDTH = 1024
BLOCK = 128
BLOCKS = TOKENS // BLOCK
HEADS = 3
HDIM = 64
INNER = HEADS * HDIM
FEED = 256
QUERY_BLOCK = 256
NORM_EPS = 1e-05
ROPE_BASE = 10000.0
MASKED = -1e30
VMEM_BYTES = 60 * 1024 * 1024

CONV_END = 512
GATE_AT = 512
QK_AT = 768
SV_AT = 896
PACKED = 1024

F32 = jnp.float32
BF16 = jnp.bfloat16


def dot(a, b):
    return lax.dot_general(a, b, (((1,), (0,)), ((), ())), preferred_element_type=F32)


def dot_right(a, b):
    return lax.dot_general(a, b, (((1,), (1,)), ((), ())), preferred_element_type=F32)


def dot_left(a, b):
    return lax.dot_general(a, b, (((0,), (0,)), ((), ())), preferred_element_type=F32)


def parts_of(values, terms):
    parts = []
    for _ in range(terms - 1):
        part = values.astype(BF16)
        parts.append(part)
        values = values - part.astype(F32)
    parts.append(values.astype(BF16))
    return parts


def times_ones(values, ones, terms=2):
    return sum(dot(part, ones) for part in parts_of(values, terms))


def ones_times(ones, values, terms=2):
    return sum(dot(ones, part) for part in parts_of(values, terms))


def iota(shape, dim):
    return lax.broadcasted_iota(jnp.int32, shape, dim)


def softplus(v):
    return jnp.maximum(v, 0.0) + jnp.log1p(jnp.exp(-jnp.abs(v)))


def sigmoid(v):
    return 1.0 / (1.0 + jnp.exp(-v))


def head_matrices():
    lane, channel = (iota((BLOCK, 256), 0), iota((BLOCK, 256), 1))
    spread = ((channel >> 6) == lane) & (channel < INNER)
    lane, channel = (iota((256, BLOCK), 1), iota((256, BLOCK), 0))
    gather = ((channel >> 6) == lane) & (channel < INNER)
    return (spread.astype(BF16), gather.astype(BF16))


def per_head(values):
    of_head = iota(values.shape, 1) >> 6
    return jnp.concatenate(
        [jnp.where(of_head == h, values, jnp.zeros_like(values)) for h in range(HEADS)], axis=0
    )


def conv_parts(proj_ref, taps_ref, aux, start):
    here = proj_ref[pl.ds(start, BLOCK), 0:CONV_END]
    before = proj_ref[pl.ds(pl.multiple_of(jnp.maximum(start - 8, 0), 8), 8), 0:CONV_END]
    both = jnp.concatenate([before, here], axis=0)
    lagged = [here]
    for lag in range(1, 4):
        lagged.append(both[8 - lag : 8 - lag + BLOCK] * aux[:, lag : lag + 1])
    pre = sum(lagged[lag] * taps_ref[lag : lag + 1, :] for lag in range(4))
    return (lagged, pre)


def step_parts(proj_ref, par_ref, aux, lower, start):
    raw = proj_ref[pl.ds(start, BLOCK), SV_AT:PACKED] + par_ref[0:1, 0:128]
    is_head = iota((BLOCK, 128), 1) < HEADS
    step = jnp.where(is_head, softplus(raw), 0.0)
    rate = -step * jnp.exp(par_ref[1:2, 0:128])
    total = ones_times(lower, rate, 3)
    reach = aux[:, 4:5] * jnp.exp(total)
    to_end = aux[:, 5:6] * jnp.exp(total[BLOCK - 1 : BLOCK, :] - total)
    return (raw, is_head, step, rate, total, reach, to_end)


def decay_of(total, total_rows, keep, h):
    gap = total[:, h : h + 1] - total_rows[h : h + 1, :]
    return jnp.exp(jnp.where(keep, gap, MASKED))


def turn_halves(values, rope, back):
    up = pltpu.roll(values, 96, 1) * rope[:, 128:256]
    down = pltpu.roll(values, 32, 1) * rope[:, 256:384]
    here = values * rope[:, 0:128]
    return here - up - down if back else here + up + down


def allowed_keys(aux_ref, segrow_ref, first, count):
    query_seg = aux_ref[first : first + QUERY_BLOCK, 0:1]
    key_seg = segrow_ref[0:1, 0:count]
    shape = (QUERY_BLOCK, count)
    return (query_seg == key_seg) & (iota(shape, 1) <= iota(shape, 0) + first)


def mixer_forward_kernel(
    normed_ref,
    w1_ref,
    w2_ref,
    aux_ref,
    segrow_ref,
    par_ref,
    taps_ref,
    rope_ref,
    mix_ref,
    proj_ref,
    states_ref,
    qkv_ref,
    lse_ref,
    heads_ref,
):
    for first in range(0, TOKENS, 256):
        rows = slice(first, first + 256)
        proj_ref[rows, :] = dot(normed_ref[rows, :], w1_ref[...])
    lane = iota((256, 128), 1)
    for first in range(0, TOKENS, 256):
        rows = slice(first, first + 256)
        turned = turn_halves(proj_ref[rows, QK_AT:SV_AT], rope_ref[rows, :], False)
        qkv_ref[rows, 0:128] = jnp.where(lane < 64, turned * AHDIM**-0.5, 0.0).astype(BF16)
        qkv_ref[rows, 128:256] = jnp.where(lane < 64, pltpu.roll(turned, 64, 1), 0.0).astype(BF16)
        tail = proj_ref[rows, SV_AT:PACKED]
        ones = jnp.where(lane == 0, 1.0, 0.0)
        qkv_ref[rows, 256:384] = jnp.where(lane >= 64, tail, ones).astype(BF16)
    for first in range(0, TOKENS, QUERY_BLOCK):
        rows = slice(first, first + QUERY_BLOCK)
        count = first + QUERY_BLOCK
        scores = dot_right(qkv_ref[rows, 0:128], qkv_ref[0:count, 128:256])
        scores = jnp.where(allowed_keys(aux_ref, segrow_ref, first, count), scores, MASKED)
        top = jnp.max(scores, axis=1, keepdims=True)
        raised = jnp.exp(scores - top)
        summed = dot(raised.astype(BF16), qkv_ref[0:count, 256:384])
        total = summed[:, 0:1]
        heads_ref[rows, 128:256] = jnp.where(lane >= 64, summed / total, 0.0).astype(BF16)
        lse_ref[rows, :] = jnp.broadcast_to(top + jnp.log(total), (QUERY_BLOCK, 128))

    spread, _ = head_matrices()
    causal = iota((BLOCK, BLOCK), 0) >= iota((BLOCK, BLOCK), 1)
    lower = causal.astype(BF16)

    def block_step(index, state):
        start = pl.multiple_of(index * BLOCK, BLOCK)
        rows = pl.ds(start, BLOCK)
        aux = aux_ref[rows, :]
        _, pre = conv_parts(proj_ref, taps_ref, aux, start)
        conv = (pre * sigmoid(pre)).astype(BF16)
        in_map, out_map, inner = (conv[:, 0:128], conv[:, 128:256], conv[:, 256:512].astype(F32))
        _, _, step, _, total, reach, to_end = step_parts(proj_ref, par_ref, aux, lower, start)
        wide = times_ones(jnp.concatenate([step, reach, to_end], axis=0), spread)
        step_wide, reach_wide, end_wide = (wide[0:128], wide[128:256], wide[256:384])
        stepped = inner * step_wide
        keep = causal & (aux[:, 0:1] == segrow_ref[0:1, pl.ds(start, BLOCK)])
        total_rows = jnp.transpose(total)
        shared = dot_right(out_map, in_map)
        mixing = jnp.concatenate(
            [(decay_of(total, total_rows, keep, h) * shared).astype(BF16) for h in range(HEADS)],
            axis=1,
        )
        states_ref[rows, :] = state
        result = dot(mixing, per_head(stepped).astype(BF16))
        result = result + dot(out_map, state.astype(BF16)) * reach_wide
        result = result + inner * par_ref[2:3, :]
        gate = proj_ref[rows, GATE_AT:QK_AT]
        gated = (result * (gate * sigmoid(gate))).astype(BF16)
        heads_ref[rows, 0:128] = gated[:, 0:128]
        heads_ref[rows, 128:256] = heads_ref[rows, 128:256] + gated[:, 128:256]
        added = dot_left(in_map, (stepped * end_wide).astype(BF16))
        return state * reach_wide[BLOCK - 1 : BLOCK, :] + added

    lax.fori_loop(0, BLOCKS, block_step, jnp.zeros((BLOCK, 256), F32))
    for first in range(0, TOKENS, 256):
        rows = slice(first, first + 256)
        mix_ref[rows, :] = dot_right(heads_ref[rows, :], w2_ref[...]).astype(BF16)


def mixer_backward_kernel(
    mixgrad_ref,
    w2_ref,
    w1_ref,
    normed_ref,
    aux_ref,
    segrow_ref,
    par_ref,
    taps_ref,
    rope_ref,
    proj_ref,
    states_ref,
    qkv_ref,
    lse_ref,
    dproj_ref,
    ngrad_ref,
    small_ref,
    gain_ref,
    d_ref,
    dkv_ref,
):
    for first in range(0, TOKENS, 256):
        rows = slice(first, first + 256)
        d_ref[rows, :] = dot(mixgrad_ref[rows, :], w2_ref[...])
    lane = iota((QUERY_BLOCK, 128), 1)
    dkv_ref[...] = jnp.zeros_like(dkv_ref)
    for first in range(0, TOKENS, QUERY_BLOCK):
        rows = slice(first, first + QUERY_BLOCK)
        count = first + QUERY_BLOCK
        queries, keys = (qkv_ref[rows, 0:128], qkv_ref[0:count, 128:256])
        out_grad = jnp.where(lane >= 64, d_ref[rows, 128:256], 0.0).astype(BF16)
        scores = dot_right(queries, keys) - lse_ref[rows, 0:1]
        weights = jnp.exp(
            jnp.where(allowed_keys(aux_ref, segrow_ref, first, count), scores, MASKED)
        )
        weight_grad = dot_right(out_grad, qkv_ref[0:count, 256:384])
        mean = jnp.sum(weights * weight_grad, axis=1, keepdims=True)
        score_grad = (weights * (weight_grad - mean)).astype(BF16)
        query_grad = dot(score_grad, keys) * AHDIM**-0.5
        d_ref[rows, 128:256] = jnp.where(
            lane < 64, d_ref[rows, 128:256], pltpu.roll(query_grad, 64, 1)
        )
        dkv_ref[0:count, 0:128] += dot_left(score_grad, queries)
        dkv_ref[0:count, 128:256] += dot_left(weights.astype(BF16), out_grad)
    for first in range(0, TOKENS, 256):
        rows = slice(first, first + 256)
        query_grad = pltpu.roll(d_ref[rows, 128:256], 64, 1)
        both = jnp.where(lane < 64, query_grad, pltpu.roll(dkv_ref[rows, 0:128], 64, 1))
        dproj_ref[rows, QK_AT:SV_AT] = turn_halves(both, rope_ref[rows, :], True).astype(BF16)
        dproj_ref[rows, SV_AT:PACKED] = jnp.where(lane >= 64, dkv_ref[rows, 128:256], 0.0).astype(
            BF16
        )

    spread, gather = head_matrices()
    row, column = (iota((BLOCK, BLOCK), 0), iota((BLOCK, BLOCK), 1))
    causal = row >= column
    lower = causal.astype(BF16)
    upper = (row <= column).astype(BF16)
    strict = (row > column).astype(BF16)
    real = iota((BLOCK, 256), 1) < INNER
    head_lane = iota((BLOCK, 128), 1)

    def block_step(turn, carried):
        state_grad, later, taps_sum, head_sum, skip_sum = carried
        start = pl.multiple_of((BLOCKS - 1 - turn) * BLOCK, BLOCK)
        rows = pl.ds(start, BLOCK)
        aux = aux_ref[rows, :]
        lagged, pre = conv_parts(proj_ref, taps_ref, aux, start)
        sig = sigmoid(pre)
        conv = (pre * sig).astype(BF16)
        in_map, out_map, inner = (conv[:, 0:128], conv[:, 128:256], conv[:, 256:512].astype(F32))
        raw, is_head, step, rate, total, reach, to_end = step_parts(
            proj_ref, par_ref, aux, lower, start
        )
        wide = times_ones(jnp.concatenate([step, reach, to_end], axis=0), spread)
        step_wide, reach_wide, end_wide = (wide[0:128], wide[128:256], wide[256:384])
        stepped = inner * step_wide
        stepped_low = stepped.astype(BF16)
        keep = causal & (aux[:, 0:1] == segrow_ref[0:1, pl.ds(start, BLOCK)])
        total_rows = jnp.transpose(total)
        shared = dot_right(out_map, in_map)
        decays = [decay_of(total, total_rows, keep, h) for h in range(HEADS)]
        mixing = [(decay * shared).astype(BF16) for decay in decays]
        state = states_ref[rows, :]
        state_low = state.astype(BF16)
        incoming = dot(out_map, state_low) * reach_wide
        result = dot(jnp.concatenate(mixing, axis=1), per_head(stepped).astype(BF16)) + incoming
        result = result + inner * par_ref[2:3, :]

        gate = proj_ref[rows, GATE_AT:QK_AT]
        gate_sig = sigmoid(gate)
        gated_grad = jnp.where(real, d_ref[rows, :], 0.0)
        gate_grad = gated_grad * result * (gate_sig * (1.0 + gate * (1.0 - gate_sig)))
        dproj_ref[rows, GATE_AT:QK_AT] = gate_grad.astype(BF16)
        out_grad = gated_grad * (gate * gate_sig)
        by_head = per_head(out_grad).astype(BF16)

        mixing_grad = dot_right(by_head, stepped_low)
        shared_grad = jnp.zeros((BLOCK, BLOCK), F32)
        edges = []
        for h in range(HEADS):
            decayed = mixing_grad[h * BLOCK : (h + 1) * BLOCK] * decays[h]
            shared_grad = shared_grad + decayed
            edges.append((decayed * shared).astype(BF16))
        crossing = dot(upper, jnp.concatenate(edges, axis=1))
        rate_grad = jnp.zeros((BLOCK, 128), F32)
        for h in range(HEADS):
            part = jnp.where(row > column, crossing[:, h * BLOCK : (h + 1) * BLOCK], 0.0)
            part = jnp.sum(part, axis=1, keepdims=True)
            rate_grad = rate_grad + jnp.where(head_lane == h, part, 0.0)

        reached = (out_grad * reach_wide).astype(BF16)
        state_grad_low = state_grad.astype(BF16)
        ended = dot(in_map, state_grad_low) * end_wide
        mapped = dot_left(jnp.concatenate(mixing, axis=0), by_head) + ended
        inner_grad = mapped * step_wide + out_grad * par_ref[2:3, :]
        kept = jnp.sum(state_grad * state, axis=0, keepdims=True)
        kept = jnp.broadcast_to(kept * reach_wide[BLOCK - 1 : BLOCK, :], (8, 256))
        sums = times_ones(
            jnp.concatenate([inner * mapped, out_grad * incoming, stepped * ended, kept], axis=0),
            gather,
        )
        flows = ones_times(
            jnp.concatenate([upper, strict], axis=1), sums[128:384]
        )
        rate_grad = rate_grad + flows + sums[384:385]
        step_grad = sums[0:128] - jnp.exp(par_ref[1:2, 0:128]) * rate_grad
        step_grad = jnp.where(is_head, step_grad * sigmoid(raw), 0.0)
        dproj_ref[rows, SV_AT:PACKED] = dproj_ref[rows, SV_AT:PACKED] + step_grad.astype(BF16)
        head_sum = head_sum + jnp.concatenate(
            [
                jnp.sum(jnp.where(is_head, rate_grad * rate, 0.0), axis=0, keepdims=True),
                jnp.sum(step_grad, axis=0, keepdims=True),
                jnp.zeros((6, 128), F32),
            ],
            axis=0,
        )
        skip_sum = skip_sum + jnp.sum(inner * out_grad, axis=0, keepdims=True)

        shared_low = shared_grad.astype(BF16)
        out_map_grad = dot(shared_low, in_map) + dot_right(reached, state_low)
        in_map_grad = dot_left(shared_low, out_map) + dot_right(
            (stepped * end_wide).astype(BF16), state_grad_low
        )
        conv_grad = jnp.concatenate([in_map_grad, out_map_grad, inner_grad], axis=1)
        pre_grad = conv_grad * (sig * (1.0 + pre * (1.0 - sig)))
        taps_sum = taps_sum + jnp.concatenate(
            [jnp.sum(pre_grad * lagged[lag], axis=0, keepdims=True) for lag in range(4)]
            + [jnp.zeros((4, CONV_END), F32)],
            axis=0,
        )
        both = jnp.concatenate([pre_grad, later], axis=0)
        masks = aux_ref[pl.ds(start, BLOCK + 8), :]
        u_grad = pre_grad * taps_ref[0:1, :]
        for lag in range(1, 4):
            shifted = (both * masks[:, lag : lag + 1])[lag : lag + BLOCK]
            u_grad = u_grad + shifted * taps_ref[lag : lag + 1, :]
        dproj_ref[rows, 0:CONV_END] = u_grad.astype(BF16)
        state_grad = state_grad * reach_wide[BLOCK - 1 : BLOCK, :] + dot_left(out_map, reached)
        return (state_grad, pre_grad[0:8], taps_sum, head_sum, skip_sum)

    carried = (
        jnp.zeros((BLOCK, 256), F32),
        jnp.zeros((8, CONV_END), F32),
        jnp.zeros((8, CONV_END), F32),
        jnp.zeros((8, 128), F32),
        jnp.zeros((1, 256), F32),
    )
    _, _, taps_sum, head_sum, skip_sum = lax.fori_loop(0, BLOCKS, block_step, carried)
    small_ref[0:8, :] = taps_sum
    small_ref[8:16, 0:128] = head_sum
    small_ref[8:16, 128:256] = jnp.zeros((8, 128), F32)
    small_ref[8:16, 256:512] = jnp.broadcast_to(skip_sum, (8, 256))

    gain = jnp.zeros((1, WIDTH), F32)
    for first in range(0, TOKENS, 256):
        rows = slice(first, first + 256)
        grad = dot_right(dproj_ref[rows, :], w1_ref[...])
        ngrad_ref[rows, :] = grad.astype(BF16)
        gain = gain + jnp.sum(grad * normed_ref[rows, :].astype(F32), axis=0, keepdims=True)
    gain_ref[...] = jnp.broadcast_to(gain, (8, WIDTH))


def feed_kernel(
    normed_ref, cot_ref, w_ref, out_ref, ngrad_ref, act_ref, grads_ref, gain_ref
):
    both = dot(normed_ref[...], w_ref[:, 256:768])
    gate, up = (both[:, 0:FEED], both[:, FEED:])
    sig = sigmoid(gate)
    silu = gate * sig
    act = (silu * up).astype(BF16)
    act_ref[...] = act
    out_ref[...] = dot_right(act, w_ref[:, 768:1024]).astype(BF16)
    act_grad = dot(cot_ref[...], w_ref[:, 768:1024])
    gate_grad = (act_grad * up * (sig + silu * (1.0 - sig))).astype(BF16)
    up_grad = (act_grad * silu).astype(BF16)
    grads = jnp.concatenate([gate_grad, up_grad], axis=1)
    grads_ref[...] = grads
    normed_grad = dot_right(grads, w_ref[:, 256:768])
    ngrad_ref[...] = normed_grad.astype(BF16)
    gain = jnp.sum(normed_grad * normed_ref[...].astype(F32), axis=0, keepdims=True)

    @pl.when(pl.program_id(0) == 0)
    def _():
        gain_ref[...] = jnp.zeros_like(gain_ref)

    gain_ref[...] += jnp.broadcast_to(gain, (8, WIDTH))


def shape_of(rows, columns, dtype):
    return jax.ShapeDtypeStruct((rows, columns), dtype)


def whole(rows, columns):
    return pl.BlockSpec((rows, columns), lambda i: (0, 0))


def mixer_forward(normed, w1, w2, aux, segrow, par, taps, rope):
    return pl.pallas_call(
        mixer_forward_kernel,
        grid=(1,),
        in_specs=[
            whole(TOKENS, WIDTH),
            whole(WIDTH, PACKED),
            whole(WIDTH, 256),
            whole(TOKENS + 8, 128),
            whole(8, TOKENS),
            whole(8, 256),
            whole(8, CONV_END),
            whole(TOKENS, 384),
        ],
        out_specs=[
            whole(TOKENS, WIDTH),
            whole(TOKENS, PACKED),
            whole(TOKENS, 256),
            whole(TOKENS, 384),
            whole(TOKENS, 128),
            whole(TOKENS, 256),
        ],
        out_shape=[
            shape_of(TOKENS, WIDTH, BF16),
            shape_of(TOKENS, PACKED, F32),
            shape_of(TOKENS, 256, F32),
            shape_of(TOKENS, 384, BF16),
            shape_of(TOKENS, 128, F32),
            shape_of(TOKENS, 256, BF16),
        ],
        compiler_params=pltpu.CompilerParams(vmem_limit_bytes=VMEM_BYTES),
        name="mixer_forward",
    )(normed, w1, w2, aux, segrow, par, taps, rope)


def mixer_backward(
    mixgrad, w2, w1, normed, aux, segrow, par, taps, rope, proj, states, qkv, lse
):
    return pl.pallas_call(
        mixer_backward_kernel,
        grid=(1,),
        in_specs=[
            whole(TOKENS, WIDTH),
            whole(WIDTH, 256),
            whole(WIDTH, PACKED),
            whole(TOKENS, WIDTH),
            whole(TOKENS + 8, 128),
            whole(8, TOKENS),
            whole(8, 256),
            whole(8, CONV_END),
            whole(TOKENS, 384),
            whole(TOKENS, PACKED),
            whole(TOKENS, 256),
            whole(TOKENS, 384),
            whole(TOKENS, 128),
        ],
        out_specs=[
            whole(TOKENS, PACKED),
            whole(TOKENS, WIDTH),
            whole(16, CONV_END),
            whole(8, WIDTH),
        ],
        out_shape=[
            shape_of(TOKENS, PACKED, BF16),
            shape_of(TOKENS, WIDTH, BF16),
            shape_of(16, CONV_END, F32),
            shape_of(8, WIDTH, F32),
        ],
        scratch_shapes=[pltpu.VMEM((TOKENS, 256), F32), pltpu.VMEM((TOKENS, 256), F32)],
        compiler_params=pltpu.CompilerParams(vmem_limit_bytes=VMEM_BYTES),
        name="mixer_backward",
    )(mixgrad, w2, w1, normed, aux, segrow, par, taps, rope, proj, states, qkv, lse)


def feed_forward_backward(normed, cot, w2):
    def rows(columns):
        return pl.BlockSpec((256, columns), lambda i: (i, 0))

    return pl.pallas_call(
        feed_kernel,
        grid=(TOKENS // 256,),
        in_specs=[rows(WIDTH), rows(WIDTH), whole(WIDTH, 1024)],
        out_specs=[rows(WIDTH), rows(WIDTH), rows(FEED), rows(2 * FEED), whole(8, WIDTH)],
        out_shape=[
            shape_of(TOKENS, WIDTH, BF16),
            shape_of(TOKENS, WIDTH, BF16),
            shape_of(TOKENS, FEED, BF16),
            shape_of(TOKENS, 2 * FEED, BF16),
            shape_of(8, WIDTH, F32),
        ],
        compiler_params=pltpu.CompilerParams(vmem_limit_bytes=VMEM_BYTES),
        name="feed",
    )(normed, cot, w2)


def aux_arrays(segments):
    seg = segments.reshape(TOKENS)
    columns = [seg.astype(F32)]
    for lag in range(1, 4):
        earlier = jnp.concatenate([jnp.full((lag,), -1, jnp.int32), seg[: TOKENS - lag]])
        columns.append((earlier == seg).astype(F32))
    ends = seg.reshape(BLOCKS, BLOCK)[:, -1]
    before = jnp.concatenate([jnp.full((1,), -1, jnp.int32), ends[:-1]])
    columns.append((seg == jnp.repeat(before, BLOCK)).astype(F32))
    columns.append((seg == jnp.repeat(ends, BLOCK)).astype(F32))
    aux = jnp.pad(jnp.stack(columns, axis=1), ((0, 8), (0, 128 - len(columns))))
    return (aux, jnp.broadcast_to(seg.astype(F32), (8, TOKENS)))


def rope_arrays():
    half = AHDIM // 2
    freq = ROPE_BASE ** (-2.0 * jnp.arange(half, dtype=F32) / AHDIM)
    angles = jnp.arange(TOKENS, dtype=F32)[:, None] * freq[None, :]
    cosine, sine = (jnp.cos(angles), jnp.sin(angles))
    none = jnp.zeros_like(sine)
    return jnp.concatenate([cosine] * 4 + [-sine, none] * 2 + [none, sine] * 2, axis=1)


def pad_columns(values, width):
    return jnp.pad(values, ((0, 0), (0, width - values.shape[1])))


def row_norm(values):
    return lax.rsqrt(jnp.mean(values * values, axis=-1, keepdims=True) + NORM_EPS)


def norm_back(values, gain, grad):
    scale = row_norm(values)
    scaled = grad * gain
    return scale * scaled - values * (
        scale**3 * jnp.mean(scaled * values, axis=-1, keepdims=True)
    )


def spread_rows(shard, axis):
    copies = jnp.broadcast_to(shard, (lax.axis_size(axis), *shard.shape))
    blocks = lax.all_to_all(copies, axis, split_axis=0, concat_axis=0, tiled=True)
    return blocks.reshape(-1, *shard.shape[1:])


def sum_rows(values, axis):
    size = lax.axis_size(axis)
    blocks = values.reshape(size, -1, values.shape[-1])
    blocks = lax.all_to_all(blocks, axis, split_axis=0, concat_axis=0, tiled=True)
    return jnp.sum(blocks.astype(F32), axis=0)


def body(
    block_input,
    segments,
    first_gain,
    mamba_gate,
    mamba_input,
    step_weight,
    state_weight,
    conv_inner,
    conv_state,
    decay_log,
    step_bias,
    skip_scale,
    query_weight,
    keyval_weight,
    mamba_out,
    attention_out,
    second_gain,
    feed_gate,
    feed_up,
    feed_down,
    cotangent,
):
    tensor_index = lax.axis_index("tensor")
    kv_head = tensor_index // (QHEADS // KVHEADS)
    aux, segrow = aux_arrays(segments)
    rope = rope_arrays()
    par = jnp.concatenate(
        [
            pad_columns(step_bias[None], 256),
            pad_columns(decay_log[None], 256),
            pad_columns(jnp.repeat(skip_scale, HDIM)[None], 256),
            jnp.zeros((5, 256), F32),
        ],
        axis=0,
    )
    taps = jnp.pad(jnp.concatenate([conv_state, pad_columns(conv_inner, 256)], axis=1), ((0, 4), (0, 0)))

    x = block_input[0].astype(F32)
    normed_here = (x * row_norm(x) * first_gain).astype(BF16)
    normed = spread_rows(normed_here, "tensor")
    shared = spread_rows(jnp.concatenate([state_weight, keyval_weight], axis=1), "tensor")
    share_rows = shared.shape[0]
    key_part = lax.dynamic_slice(shared, (0, 256 + kv_head * AHDIM), (share_rows, AHDIM))
    value_part = lax.dynamic_slice(
        shared, (0, 256 + (KVHEADS + kv_head) * AHDIM), (share_rows, AHDIM)
    )
    w1_here = jnp.concatenate(
        [
            shared[:, 0:256],
            pad_columns(mamba_input, 256),
            pad_columns(mamba_gate, 256),
            query_weight,
            key_part,
            pad_columns(step_weight, 64),
            value_part,
        ],
        axis=1,
    )
    w2_here = jnp.concatenate(
        [mamba_out.T, attention_out.T, feed_gate, feed_up, feed_down.T], axis=1
    )
    w1 = lax.all_gather(w1_here, "dp", axis=0, tiled=True)
    w2 = lax.all_gather(w2_here, "dp", axis=0, tiled=True)

    mix, proj, states, qkv, lse, heads = mixer_forward(
        normed, w1, w2, aux, segrow, par, taps, rope
    )
    hidden = x + sum_rows(mix, "tensor")
    normed_two = spread_rows((hidden * row_norm(hidden) * second_gain).astype(BF16), "tensor")
    cot_all = spread_rows(cotangent[0], "tensor")
    out_part, normed_two_grad, act, feed_grads, second_part = feed_forward_backward(
        normed_two, cot_all, w2
    )
    block_out = hidden + sum_rows(out_part, "tensor")
    hidden_grad = cotangent[0].astype(F32) + norm_back(
        hidden, second_gain, sum_rows(normed_two_grad, "tensor")
    )
    mix_grad = spread_rows(hidden_grad.astype(BF16), "tensor")
    dproj, normed_grad, small, first_part = mixer_backward(
        mix_grad, w2, w1, normed, aux, segrow, par, taps, rope, proj, states, qkv, lse
    )
    w2_grad = jnp.concatenate(
        [
            dot_left(mix_grad, heads).astype(BF16),
            dot_left(normed_two, feed_grads).astype(BF16),
            dot_left(cot_all, act).astype(BF16),
        ],
        axis=1,
    )
    w1_grad = dot_left(normed, dproj).astype(BF16)
    input_grad = hidden_grad + norm_back(x, first_gain, sum_rows(normed_grad, "tensor"))

    w2_sum = sum_rows(w2_grad, "dp")
    w1_sum = sum_rows(w1_grad, "dp")
    shared_sum = jnp.zeros((share_rows, 512), F32)
    shared_sum = lax.dynamic_update_slice(shared_sum, w1_sum[:, 0:256], (0, 0))
    shared_sum = lax.dynamic_update_slice(
        shared_sum, w1_sum[:, 832:896], (0, 256 + kv_head * AHDIM)
    )
    shared_sum = lax.dynamic_update_slice(
        shared_sum, w1_sum[:, 960:1024], (0, 256 + (KVHEADS + kv_head) * AHDIM)
    )
    shared_sum = sum_rows(shared_sum, "tensor")

    tensor_count = lax.axis_size("tensor")
    own = jnp.concatenate(
        [
            small[0:4, 256 : 256 + INNER].reshape(-1),
            small[8, 0:HEADS],
            small[9, 0:HEADS],
            jnp.sum(small[8, 256 : 256 + INNER].reshape(HEADS, HDIM), axis=1),
        ]
    )
    own_all = lax.dynamic_update_slice(
        jnp.zeros((tensor_count, own.shape[0]), F32), own[None], (tensor_index, 0)
    )
    first_sum, second_sum, state_taps_sum, own_sum = lax.psum(
        (first_part[0] / first_gain, second_part[0] / second_gain, small[0:4, 0:256], own_all),
        ("dp", "tensor"),
    )
    own = lax.dynamic_slice(own_sum, (tensor_index, 0), (1, own.shape[0]))[0]
    taps_end = 4 * INNER
    return (
        block_out.astype(BF16)[None],
        input_grad[None],
        first_sum,
        w1_sum[:, GATE_AT : GATE_AT + INNER],
        w1_sum[:, 256 : 256 + INNER],
        w1_sum[:, SV_AT : SV_AT + HEADS],
        shared_sum[:, 0:256],
        own[0:taps_end].reshape(4, INNER),
        state_taps_sum,
        own[taps_end : taps_end + HEADS],
        own[taps_end + HEADS : taps_end + 2 * HEADS],
        own[taps_end + 2 * HEADS :],
        w1_sum[:, QK_AT : QK_AT + AHDIM],
        shared_sum[:, 256:512],
        w2_sum[:, 0:INNER].T,
        w2_sum[:, INNER:256].T,
        second_sum,
        w2_sum[:, 256:512],
        w2_sum[:, 512:768],
        w2_sum[:, 768:1024].T,
    )


def solution(mesh):
    in_specs = (
        P("dp", "tensor", None),
        P("dp", None),
        P(),
        P("dp", "tensor"),
        P("dp", "tensor"),
        P("dp", "tensor"),
        P(("dp", "tensor"), None),
        P(None, "tensor"),
        P(),
        P("tensor"),
        P("tensor"),
        P("tensor"),
        P("dp", "tensor"),
        P(("dp", "tensor"), None),
        P("tensor", "dp"),
        P("tensor", "dp"),
        P(),
        P("dp", "tensor"),
        P("dp", "tensor"),
        P("tensor", "dp"),
        P("dp", "tensor", None),
    )
    out_specs = (
        P("dp", "tensor", None),
        P("dp", "tensor", None),
        P(),
        P("dp", "tensor"),
        P("dp", "tensor"),
        P("dp", "tensor"),
        P(("dp", "tensor"), None),
        P(None, "tensor"),
        P(),
        P("tensor"),
        P("tensor"),
        P("tensor"),
        P("dp", "tensor"),
        P(("dp", "tensor"), None),
        P("tensor", "dp"),
        P("tensor", "dp"),
        P(),
        P("dp", "tensor"),
        P("dp", "tensor"),
        P("tensor", "dp"),
    )
    return jax.shard_map(body, mesh=mesh, in_specs=in_specs, out_specs=out_specs, check_vma=False)
```

time: 1790 us -> 504 us (0.28); the launches traced: 1770 us -> 502 us
  waiting for transfers between devices: 783 us -> 122 us
  local copies, waits for them, and re-layouts: 413 us -> 38 us
  matrix products: 239 us -> 9.3 us
  other arithmetic: 180 us -> 19.2 us
  blocking collectives: 97.6 us -> 204 us
  Pallas kernels: 0 us -> 54.1 us
  starting transfers between devices: 16.9 us -> 40.6 us
  loops' own time: 22.3 us -> 0 us
    all_gather x2, waiting for transfers between devices: 317 us -> 33.8 us  [the longest x1 33.8 us: body(): w1 = lax.all_gather(w1_here, 'dp', axis=0, tiled=True)]
    dot_general x146 -> x4, matrix products: 239 us -> 9.3 us  [dot_left(): lax.dot_general(a, b, (((0,), (0,)), ((), ())), preferred_element_type=F32)]
    reduce_scatter x4 -> x0, waiting for transfers between devices: 208 us -> none  [the longest x1 75.9 us: body(): lax.psum_scatter(mix_terms.reshape(row_count, length, model_width).astype...]
    unnamed x9 -> x2, waiting for transfers between devices: 125 us -> 0.03 us
    dynamic_update_slice x76 -> x3, local copies, waits for them, and re-layouts: 119 us -> 2.88 us  [the longest x1 1.41 us: body(): lax.dynamic_update_slice(shared_sum, w1_sum[:, 832:896], (0, 256 + kv_hea...]
    psum x1 -> x0, waiting for transfers between devices: 108 us -> none  [body(): lax.psum((state_grad, keyval_grad_full, first_gain_grad, second_gain_grad...]
    all_to_all x1 -> x4, blocking collectives: 31 us -> 121 us  [the longest x2 64 us: sum_rows(): lax.all_to_all(blocks, axis, split_axis=0, concat_axis=0, tiled=True)]
    squeeze x73 -> x1, local copies, waits for them, and re-layouts: 78 us -> 0.77 us  [body(): small[8, 0:HEADS]]
  transfers between devices with their start and end apart: 11 -> 10, of which waited for: 10 -> 7; matrix products, arithmetic and copies ran while one was open for 7% -> 10% of each run, Pallas kernels for 0% -> 6%
where the time goes in v1:
time: 504 us; the launch traced here: 502 us
  blocking collectives  204 us (40%)
  waiting for transfers between devices  122 us (24%)
  Pallas kernels  54.1 us (11%)
  starting transfers between devices  40.6 us (8%)
  local copies, waits for them, and re-layouts  38 us (8%)
  other arithmetic  19.2 us (4%)
  between operations  14.5 us (3%)
  matrix products  9.3 us (2%)
    psum x1, blocking collectives, body(): lax.psum((first_part[0] / first_gain, second_part[0] / second_gain, small...  83.1 us
    all_to_all x2, blocking collectives, sum_rows(): lax.all_to_all(blocks, axis, split_axis=0, concat_axis=0, tiled=True)  64 us
    all_to_all x2, blocking collectives, spread_rows(): lax.all_to_all(copies, axis, split_axis=0, concat_axis=0, tiled=True)  57.4 us
    all_to_all x3, waiting for transfers between devices, spread_rows(): lax.all_to_all(copies, axis, split_axis=0, concat_axis=0, tiled=True)  49 us
    all_to_all x5, waiting for transfers between devices, sum_rows(): lax.all_to_all(blocks, axis, split_axis=0, concat_axis=0, tiled=True)  39.2 us
    all_gather x1, waiting for transfers between devices, body(): w1 = lax.all_gather(w1_here, 'dp', axis=0, tiled=True)  33.8 us
    pallas_call x1, Pallas kernels, mixer_backward(): pl.pallas_call(mixer_backward_kernel, grid=(1,), in_specs=[whole(TOKENS,...  28.6 us
    all_to_all x5, starting transfers between devices, sum_rows(): lax.all_to_all(blocks, axis, split_axis=0, concat_axis=0, tiled=True)  25.3 us
  transfers between devices with their start and end apart: 10, of which 7 were waited for; matrix products, arithmetic and copies ran while one was open for 10% of the time, Pallas kernels for 6%

profile of v1, /device:TPU:0, one launch (start us, length us, event | category | flops | bytes accessed | tf_op | source)
XLA Modules:
  0.0 502.2 jit_solution(11797073172885636286)
XLA Ops:
  7.2 0.8 copy.72
  8.0 1.6 concatenate.50
  11.0 7.9 %all-to-all-start.1 = ((bf16[8,8,512]{2,1,0:T(8,128)(2,1)}), bf16[8,8,512]{2,1,0:T(8,128)(2,1)S(1)}, u32[]{:S(2)}, u32[]{:S(2)}) async-start(bf16[8,8,512]{2,1,0:T(8,128)(2,1)} %broadcast_in_dim.61), calls=%async_computation.1 | async-start | bytes 131072 | tf_op jit(solution)/shard_map/all_to_all | solution.py:565
  21.2 5.4 %all-to-all-done.1 = bf16[8,8,512]{2,1,0:T(8,128)(2,1)S(1)} async-done(((bf16[8,8,512]{2,1,0:T(8,128)(2,1)}), bf16[8,8,512]{2,1,0:T(8,128)(2,1)S(1)}, u32[]{:S(2)}, u32[]{:S(2)}) %all-to-all-start.1) | async-done | bytes 65568 | tf_op jit(solution)/shard_map/all_to_all | solution.py:565
  26.7 1.5 concatenate.49
  28.2 1.1 fusion.5
  29.3 1.1 fusion.7
  30.4 1.6 broadcast_in_dim.60
  32.0 3.7 all-to-all-start
  37.6 0.9 pad.40.aux_ref
  38.5 2.7 fusion.16
  41.2 0.9 concatenate.58
  42.1 0.9 broadcast_in_dim.69
  42.9 4.7 concatenate.59.rope_ref
  48.3 16.6 %all-to-all-done = bf16[8,128,1024]{2,1,0:T(8,128)(2,1)S(1)} async-done(((bf16[8,128,1024]{2,1,0:T(8,128)(2,1)}), bf16[8,128,1024]{2,1,0:T(8,128)(2,1)S(1)}, u32[]{:S(2)}, u32[]{:S(2)}) %all-to-all-start) | async-done | bytes 2097184 | tf_op jit(solution)/shard_map/all_to_all | solution.py:565
  64.9 33.8 %all-gather.3.cloned.1.call-done.w1_ref = bf16[1024,1024]{1,0:T(8,128)(2,1)} async-done(((bf16[64,1024]{1,0:T(8,128)(2,1)}), bf16[1024,1024]{1,0:T(8,128)(2,1)}) %all-gather.3.cloned.1.call-update) | async-done | bytes 2097168 | tf_op jit(solution)/shard_map/all_gather | solution.py:638
  99.3 16.2 %mixer_forward.1 = (bf16[1024,1024]{1,0:T(8,128)(2,1)}, f32[1024,1024]{1,0:T(8,128)}, f32[1024,256]{1,0:T(8,128)}, bf16[1024,384]{1,0:T(8,128)(2,1)}, f32[1024,128]{1,0:T(8,128)}, /*index=5*/bf16[1024,256]{1,0:T(8,128)(2,1)}) custom-call(bf16[1024,1024]{1,0:T(8,128)(2,1)} %bitcast.118, bf16[1024,1024]{1,0:T(8,128)(2,1)} %all-gather.3.cloned.1.call-done.w1_ref, ...), custom_call_target="tpu_custom_call" | custom-call | tf_op jit(solution)/shard_map/mixer_forward/pallas_call | solution.py:430
  115.5 35.2 %all_to_all.60 = bf16[8,128,1024]{2,1,0:T(8,128)(2,1)} all-to-all(bf16[8,128,1024]{2,1,0:T(8,128)(2,1)} %bitcast.131), channel_id=1, replica_groups=mesh['dp'=16,'tensor'=8] {'tensor'}, dimensions={0} | all-to-all | bytes 4194304 | tf_op jit(solution)/shard_map/all_to_all | solution.py:572
  150.7 1.6 broadcast_in_dim.71
  152.3 3.6 all-to-all-start.4
  155.9 2.0 convert_reduce_fusion.5
  158.3 27.0 %all-to-all-done.4 = bf16[8,128,1024]{2,1,0:T(8,128)(2,1)S(1)} async-done(((bf16[8,128,1024]{2,1,0:T(8,128)(2,1)}), bf16[8,128,1024]{2,1,0:T(8,128)(2,1)S(1)}, u32[]{:S(2)}, u32[]{:S(2)}) %all-to-all-start.4) | async-done | bytes 2097184 | tf_op jit(solution)/shard_map/all_to_all | solution.py:565
  185.6 30.1 %all_to_all.61 = bf16[8,128,1024]{2,1,0:T(8,128)(2,1)} all-to-all(bf16[8,128,1024]{2,1,0:T(8,128)(2,1)S(1)} %broadcast_in_dim.70), channel_id=1, replica_groups=mesh['dp'=16,'tensor'=8] {'tensor'}, dimensions={0} | all-to-all | bytes 4194304 | tf_op jit(solution)/shard_map/all_to_all | solution.py:565
  215.7 9.3 %feed.1 = (bf16[1024,1024]{1,0:T(8,128)(2,1)}, bf16[1024,1024]{1,0:T(8,128)(2,1)}, bf16[1024,256]{1,0:T(8,128)(2,1)}, bf16[1024,512]{1,0:T(8,128)(2,1)}, f32[8,1024]{1,0:T(8,128)}) custom-call(bf16[1024,1024]{1,0:T(8,128)(2,1)} %bitcast.123, bf16[1024,1024]{1,0:T(8,128)(2,1)} %bitcast.121, bf16[1024,1024]{1,0:T(8,128)(2,1)} %all-gather.5.cloned.1.call-done.w2_ref.w_ref), custom_call_target="tpu_custom_call" | custom-call | tf_op jit(solution)/shard_map/feed/pallas_call | solution.py:507
  225.0 28.8 %all_to_all.62 = bf16[8,128,1024]{2,1,0:T(8,128)(2,1)S(1)} all-to-all(bf16[8,128,1024]{2,1,0:T(8,128)(2,1)} %bitcast.132), channel_id=1, replica_groups=mesh['dp'=16,'tensor'=8] {'tensor'}, dimensions={0} | all-to-all | bytes 4194304 | tf_op jit(solution)/shard_map/all_to_all | solution.py:572
  254.8 27.3 %all_to_all.63 = bf16[8,128,1024]{2,1,0:T(8,128)(2,1)} all-to-all(bf16[8,128,1024]{2,1,0:T(8,128)(2,1)S(1)} %broadcast_in_dim.72), channel_id=1, replica_groups=mesh['dp'=16,'tensor'=8] {'tensor'}, dimensions={0} | all-to-all | bytes 4194304 | tf_op jit(solution)/shard_map/all_to_all | solution.py:565
  282.1 3.6 all-to-all-start.5
  285.7 28.6 %mixer_backward.1 = (bf16[1024,1024]{1,0:T(8,128)(2,1)}, bf16[1024,1024]{1,0:T(8,128)(2,1)}, f32[16,512]{1,0:T(8,128)}, f32[8,1024]{1,0:T(8,128)}) custom-call(bf16[1024,1024]{1,0:T(8,128)(2,1)} %bitcast.125, bf16[1024,1024]{1,0:T(8,128)(2,1)} %all-gather.5.cloned.1.call-done.w2_ref.w_ref, bf16[1024,1024]{1,0:T(8,128)(2,1)} %all-gather.3.cloned.1.call-done.w1_ref, ...), custom_call_target="tpu_custom_call" | custom-call | tf_op jit(solution)/shard_map/mixer_backward/pallas_call | solution.py:467
  314.3 1.3 copy-done.7
  315.7 7.3 %all-to-all-start.8 = ((bf16[8,128,1024]{2,1,0:T(8,128)(2,1)}), bf16[8,128,1024]{2,1,0:T(8,128)(2,1)}, u32[]{:S(2)}, u32[]{:S(2)}) async-start(bf16[8,128,1024]{2,1,0:T(8,128)(2,1)} %bitcast.129), calls=%async_computation.8 | async-start | bytes 4194304 | tf_op jit(solution)/shard_map/all_to_all | solution.py:572
  322.9 1.9 fusion
  324.9 1.3 convolution_convert_fusion.1
  327.6 2.7 copy.77
  330.2 16.4 %all-to-all-done.8 = bf16[8,128,1024]{2,1,0:T(8,128)(2,1)} async-done(((bf16[8,128,1024]{2,1,0:T(8,128)(2,1)}), bf16[8,128,1024]{2,1,0:T(8,128)(2,1)}, u32[]{:S(2)}, u32[]{:S(2)}) %all-to-all-start.8) | async-done | bytes 2097184 | tf_op jit(solution)/shard_map/all_to_all | solution.py:572
  346.7 4.6 all-to-all-start.11
  351.3 0.9 slice.148
  352.2 2.8 convert_reduce_fusion.4
  358.2 5.3 %convolution_convert_fusion = bf16[1024,1024]{1,0:T(8,128)(2,1)} fusion(bf16[1024,1024]{1,0:T(8,128)(2,1)S(1)} %bitcast.120, bf16[1024,1024]{1,0:T(8,128)(2,1)} %get-tuple-element.44), kind=kOutput, calls=%fused_computation.7 | convolution fusion | flops 2148532224 | bytes 6291456 | tf_op jit(solution)/shard_map/dot_general | solution.py:44
  363.5 15.5 %all-to-all-done.11 = bf16[16,64,1024]{2,1,0:T(8,128)(2,1)} async-done(((bf16[16,64,1024]{2,1,0:T(8,128)(2,1)}), bf16[16,64,1024]{2,1,0:T(8,128)(2,1)}, u32[]{:S(2)}, u32[]{:S(2)}) %all-to-all-start.11) | async-done | bytes 2097184 | tf_op jit(solution)/shard_map/all_to_all | solution.py:572
  379.0 4.7 all-to-all-start.9
  384.7 83.1 %all-reduce.11 = (f32[1024]{0:T(1024)}, f32[8,777]{1,0:T(8,128)S(1)}, f32[4,256]{1,0:T(4,128)}, f32[1024]{0:T(1024)}) all-reduce(f32[1024]{0:T(1024)S(1)} %div.57, f32[8,777]{1,0:T(8,128)S(1)} %dynamic_update_slice.15, f32[4,256]{1,0:T(4,128)S(1)} %slice.137, f32[1024]{0:T(1024)S(1)} %div.58), channel_id=1, replica_groups=mesh['dp'=16,'tensor'=8] {'dp','tensor'}, use_global_device_ids=true, to_apply=%region_8.9 | all-reduce | flops 9288 | bytes 74304 | tf_op jit(solution)/shard_map/psum | solution.py:693
  469.0 2.0 convert_reduce_fusion.2
  471.3 1.2 fusion.10
  472.5 2.0 convert_reduce_fusion
  479.0 1.4 dynamic_update_slice.13
  480.4 1.4 dynamic_update_slice.14
  481.8 5.0 %all-to-all-start.10 = ((f32[8,8,512]{2,1,0:T(8,128)}), f32[8,8,512]{2,1,0:T(8,128)S(1)}, u32[]{:S(2)}, u32[]{:S(2)}) async-start(f32[8,8,512]{2,1,0:T(8,128)} %bitcast.34), calls=%async_computation.10 | async-start | bytes 262144 | tf_op jit(solution)/shard_map/all_to_all | solution.py:572
  487.4 7.3 %all-to-all-done.10 = f32[8,8,512]{2,1,0:T(8,128)S(1)} async-done(((f32[8,8,512]{2,1,0:T(8,128)}), f32[8,8,512]{2,1,0:T(8,128)S(1)}, u32[]{:S(2)}, u32[]{:S(2)}) %all-to-all-start.10) | async-done | bytes 131104 | tf_op jit(solution)/shard_map/all_to_all | solution.py:572
  (124 shorter events, 21.2 us)
Async XLA Ops:
  7.2 57.7 %all-gather.5.cloned.1.call-start = ((), (), s32[]{:S(2)}) async-start(), calls=%async_computation.13 | async-start | bytes 2228224 | tf_op jit(solution)/shard_map/all_gather | solution.py:639
  11.0 15.6 %all-to-all-start.1 = ((bf16[8,8,512]{2,1,0:T(8,128)(2,1)}), bf16[8,8,512]{2,1,0:T(8,128)(2,1)S(1)}, u32[]{:S(2)}, u32[]{:S(2)}) async-start(bf16[8,8,512]{2,1,0:T(8,128)(2,1)} %broadcast_in_dim.61), calls=%async_computation.1 | async-start | bytes 131072 | tf_op jit(solution)/shard_map/all_to_all | solution.py:565
  18.8 79.8 %all-gather.3.cloned.1.call-start = ((), (), s32[]{:S(2)}) async-start(), calls=%async_computation.12 | async-start | bytes 2228224 | tf_op jit(solution)/shard_map/all_gather | solution.py:638
  32.0 3.8 copy-start.11
  32.0 3.9 copy-start.17
  32.0 4.9 copy-start.14
  32.0 4.9 copy-start.15
  32.0 32.8 %all-to-all-start = ((bf16[8,128,1024]{2,1,0:T(8,128)(2,1)}), bf16[8,128,1024]{2,1,0:T(8,128)(2,1)S(1)}, u32[]{:S(2)}, u32[]{:S(2)}) async-start(bf16[8,128,1024]{2,1,0:T(8,128)(2,1)} %broadcast_in_dim.60), calls=%async_computation | async-start | bytes 4194304 | tf_op jit(solution)/shard_map/all_to_all | solution.py:565
  42.9 4.7 copy-start.18
  42.9 4.7 copy-start.19
  64.8 34.5 %copy-start = (bf16[8,128,1024]{2,1,0:T(8,128)(2,1)}, bf16[8,128,1024]{2,1,0:T(8,128)(2,1)S(1)}, u32[]{:S(2)}) copy-start(bf16[8,128,1024]{2,1,0:T(8,128)(2,1)S(1)} %all-to-all-done) | copy-start | bytes 6291460
  115.5 35.2 %copy-start.8 = (bf16[1,128,1024]{2,1,0:T(8,128)(2,1)S(1)}, bf16[1,128,1024]{2,1,0:T(8,128)(2,1)}, u32[]{:S(2)}) copy-start(bf16[1,128,1024]{2,1,0:T(8,128)(2,1)} %param.41) | copy-start | bytes 786436
  152.3 33.0 %all-to-all-start.4 = ((bf16[8,128,1024]{2,1,0:T(8,128)(2,1)}), bf16[8,128,1024]{2,1,0:T(8,128)(2,1)S(1)}, u32[]{:S(2)}, u32[]{:S(2)}) async-start(bf16[8,128,1024]{2,1,0:T(8,128)(2,1)} %broadcast_in_dim.71), calls=%async_computation.4 | async-start | bytes 4194304 | tf_op jit(solution)/shard_map/all_to_all | solution.py:565
  155.9 2.1 copy-start.4
  155.9 2.2 copy-start.12
  185.3 30.4 %copy-start.2 = (bf16[8,128,1024]{2,1,0:T(8,128)(2,1)}, bf16[8,128,1024]{2,1,0:T(8,128)(2,1)S(1)}, u32[]{:S(2)}) copy-start(bf16[8,128,1024]{2,1,0:T(8,128)(2,1)S(1)} %all-to-all-done.4) | copy-start | bytes 6291460
  282.1 32.3 %all-to-all-start.5 = ((bf16[8,128,1024]{2,1,0:T(8,128)(2,1)}), bf16[8,128,1024]{2,1,0:T(8,128)(2,1)S(1)}, u32[]{:S(2)}, u32[]{:S(2)}) async-start(bf16[8,128,1024]{2,1,0:T(8,128)(2,1)} %bitcast.130), calls=%async_computation.5 | async-start | bytes 4194304 | tf_op jit(solution)/shard_map/all_to_all | solution.py:572
  314.3 1.3 copy-start.7
  315.7 7.3 %copy-start.3 = (bf16[8,128,1024]{2,1,0:T(8,128)(2,1)S(1)}, bf16[8,128,1024]{2,1,0:T(8,128)(2,1)}, u32[]{:S(2)}) copy-start(bf16[8,128,1024]{2,1,0:T(8,128)(2,1)} %copy-done.2) | copy-start | bytes 6291460
  315.7 31.0 %all-to-all-start.8 = ((bf16[8,128,1024]{2,1,0:T(8,128)(2,1)}), bf16[8,128,1024]{2,1,0:T(8,128)(2,1)}, u32[]{:S(2)}, u32[]{:S(2)}) async-start(bf16[8,128,1024]{2,1,0:T(8,128)(2,1)} %bitcast.129), calls=%async_computation.8 | async-start | bytes 4194304 | tf_op jit(solution)/shard_map/all_to_all | solution.py:572
  322.9 1.9 copy-start.5
  322.9 2.0 copy-start.20
  324.9 1.6 copy-start.6
  324.9 1.7 copy-start.21
  346.7 32.3 %all-to-all-start.11 = ((bf16[16,64,1024]{2,1,0:T(8,128)(2,1)}), bf16[16,64,1024]{2,1,0:T(8,128)(2,1)}, u32[]{:S(2)}, u32[]{:S(2)}) async-start(bf16[16,64,1024]{2,1,0:T(8,128)(2,1)} %bitcast.41), calls=%async_computation.11 | async-start | bytes 4194304 | tf_op jit(solution)/shard_map/all_to_all | solution.py:572
  351.3 6.8 %copy-start.13 = (f32[1024]{0:T(1024)S(1)}, f32[1024]{0:T(1024)}, u32[]{:S(2)}) copy-start(f32[1024]{0:T(1024)} %param.23) | copy-start | bytes 12292
  351.3 6.9 %copy-start.1 = (bf16[8,128,1024]{2,1,0:T(8,128)(2,1)S(1)}, bf16[8,128,1024]{2,1,0:T(8,128)(2,1)}, u32[]{:S(2)}) copy-start(bf16[8,128,1024]{2,1,0:T(8,128)(2,1)} %copy-done) | copy-start | bytes 6291460
  379.0 96.3 %all-to-all-start.9 = ((bf16[16,64,1024]{2,1,0:T(8,128)(2,1)}), bf16[16,64,1024]{2,1,0:T(8,128)(2,1)S(1)}, u32[]{:S(2)}, u32[]{:S(2)}) async-start(bf16[16,64,1024]{2,1,0:T(8,128)(2,1)} %bitcast.128), calls=%async_computation.9 | async-start | bytes 4194304 | tf_op jit(solution)/shard_map/all_to_all | solution.py:572
  468.5 2.8 copy-start.9
  468.5 2.8 copy-start.10
  474.5 3.8 copy-start.16
  481.8 12.9 %all-to-all-start.10 = ((f32[8,8,512]{2,1,0:T(8,128)}), f32[8,8,512]{2,1,0:T(8,128)S(1)}, u32[]{:S(2)}, u32[]{:S(2)}) async-start(f32[8,8,512]{2,1,0:T(8,128)} %bitcast.34), calls=%async_computation.10 | async-start | bytes 262144 | tf_op jit(solution)/shard_map/all_to_all | solution.py:572
Sparse Core Ops, SparseCore 0:
  9.8 53.3 all-gather.4
  65.4 33.2 all-gather.2
